TPU v7x, 128 devices: a whole 4x4x4 slice. The times are simulated.
128 devices in a mesh: row: 8 (over y, z_lo), col: 16 (over z_hi, x, core).
Axes of the slice: x: 4, y: 4, z: 4 (z_hi: 2, z_lo: 2; z = z_hi * 2 + z_lo), core: 2. Of those that a mesh axis runs over, the one named last changes fastest.
Arguments:
- velocities: bfloat16 [1024, 61440], P(None, 'row'), may hold values from -60 to 60, as said below
- modes_panel: bfloat16 [61440, 4096], P('row', 'col'), may hold values from -1 to 1
- atom_slot: int32 [20480], P('row'), may hold values from 0 to 2559, as said below
- lag_offsets: int32 [8], replicated, may hold values from 0 to 256, as said below
Outputs:
- correlations: float32 [8, 4096, 4096], P(None, 'row', 'col')
Inputs may be any that keep to these rules, and one draw needn't show every extreme that they name: `velocities`: every snapshot row has its own scale. Within each aligned block of 2560 atoms, atom_slot is a permutation of 0 to 2559. `lag_offsets`: one of the lags equals 256.
All inputs are finite; a program needn't handle non-finite values.
Results may differ from a plain program's by a relative error of at most 0.0041.
Values may be sent and summed in bfloat16 or wider, within the bound.
A program may use at most 128 MiB of HBM per device.

v0:
```python
import jax
import jax.numpy as jnp
from jax import lax
from jax.sharding import PartitionSpec as P

M = 4096
LAGS = 8
MAXLAG = 256


epsilon = 1e-06


def reorder(modes_panel, atom_slot):
    per_atom = modes_panel.reshape(atom_slot.shape[0], 3, modes_panel.shape[1])
    return jnp.take(per_atom, atom_slot, axis=0).reshape(modes_panel.shape)


def correlate(row_modes, column_modes, lag_offsets):
    snapshots = column_modes.shape[0]
    padded = jnp.concatenate(
        [column_modes, jnp.zeros((MAXLAG, column_modes.shape[1]), jnp.bfloat16)], axis=0
    )
    results = []
    for number in range(LAGS):
        offset = lag_offsets[number]
        shifted = lax.dynamic_slice_in_dim(padded, offset, snapshots, 0)
        product = lax.dot_general(
            row_modes, shifted, (((0,), (0,)), ((), ())), preferred_element_type=jnp.float32
        )
        results.append(product * lax.rsqrt((snapshots - offset).astype(jnp.float32)))
    return jnp.stack(results)


def local(velocities, modes_panel, atom_slot, lag_offsets):
    panel = reorder(modes_panel, atom_slot)
    row_count = lax.axis_size("row")
    partial_terms = jnp.dot(velocities, panel, preferred_element_type=jnp.float32)
    projected = lax.psum(partial_terms, "row")
    energy = lax.psum(jnp.sum(projected * projected, axis=1), "col")
    column_modes = (projected * lax.rsqrt(energy / M + epsilon)[:, None]).astype(jnp.bfloat16)
    block_width = M // row_count
    every_mode = lax.all_gather(column_modes, "col", axis=1, tiled=True)
    row_modes = lax.dynamic_slice_in_dim(
        every_mode, lax.axis_index("row") * block_width, block_width, 1
    )
    return correlate(row_modes, column_modes, lag_offsets)


def solution(mesh):
    return jax.shard_map(
        local,
        mesh=mesh,
        in_specs=(P(None, "row"), P("row", "col"), P("row"), P()),
        out_specs=P(None, "row", "col"),
        check_vma=False,
    )
```

profile of v0, /device:TPU:1, one launch (start us, length us, event | category | flops | bytes accessed | tf_op | source)
XLA Modules:
  0.0 265.8 jit_solution(16931310440080507958)
XLA Ops:
  6.5 0.0 all-reduce.3.cloned.1.call-start
  6.5 0.7 compare_select_fusion
  7.2 0.7 compare_and_fusion
  8.0 11.0 %reshape.12 = bf16[2560,3,256]{2,1,0:T(4,128)(2,1)} reshape(bf16[7680,256]{1,0:T(8,128)(2,1)} %param.5) | data formatting | bytes 7864320 | tf_op jit(solution)/shard_map/reshape | solution.py:15
  18.9 13.3 %gather_fusion = bf16[2560,3,256]{2,1,0:T(4,128)(2,1)} fusion(bf16[2560,3,256]{2,1,0:T(4,128)(2,1)} %reshape.12, s32[3072]{0:T(1024)S(1)} %pad_clamp_fusion), kind=kCustom, calls=%fused_computation | custom fusion | bytes 7874560 | tf_op jit(solution)/shard_map/jit(_take)/gather | solution.py:16
  32.3 10.7 %gather.7 = bf16[7680,256]{1,0:T(8,128)(2,1)} reshape(bf16[2560,3,256]{2,1,0:T(4,128)(2,1)} %gather_fusion) | data formatting | bytes 7864320 | tf_op jit(solution)/shard_map/jit(_take)/gather | solution.py:16
  42.9 1.3 broadcast_in_dim.18
  44.3 1.1 broadcast_in_dim.19
  45.3 12.0 %fusion.4 = f32[1024,256]{0,1:T(8,128)} fusion(bf16[1024,7680]{1,0:T(8,128)(2,1)} %param.4, bf16[7680,256]{1,0:T(8,128)(2,1)} %gather.7, pred[7680]{0:T(1024)(128)(4,1)S(1)} %broadcast_in_dim.19), kind=kOutput, calls=%fused_computation.5 | convolution fusion | flops 4028497920 | bytes 20717056 | tf_op jit(solution)/shard_map/dot_general | solution.py:38
  57.3 0.0 copy-start.1
  57.3 0.0 all-reduce.3.cloned.1.call-update
  57.3 0.0 all-gather.2.cloned.1.call-start
  57.4 77.0 %all-reduce.3.cloned.1.call-done = f32[1024,256]{0,1:T(8,128)} async-done(((f32[1024,256]{0,1:T(8,128)}), f32[1024,256]{0,1:T(8,128)}) %all-reduce.3.cloned.1.call-update) | async-done | bytes 1048592 | tf_op jit(solution)/shard_map/psum | solution.py:39
  134.4 1.3 multiply_reduce_fusion
  135.7 37.5 %psum.15 = f32[1024]{0:T(1024)S(1)} all-reduce(f32[1024]{0:T(1024)S(1)} %multiply_reduce_fusion), channel_id=1, replica_groups=mesh['row'=8,'col'=16] {'col'}, use_global_device_ids=true, to_apply=%region_2.3 | all-reduce | flops 1024 | bytes 8192 | tf_op jit(solution)/shard_map/psum | solution.py:40
  173.2 2.1 multiply_convert_fusion
  175.3 0.0 copy-start
  175.3 0.0 all-gather.2.cloned.1.call-update
  175.4 0.0 copy-done.1
  175.4 0.7 fusion.48
  196.7 49.1 %all-gather.2.cloned.1.call-done = bf16[1024,4096]{0,1:T(8,128)(2,1)} async-done(((bf16[1024,256]{0,1:T(8,128)(2,1)}), bf16[1024,4096]{0,1:T(8,128)(2,1)}) %all-gather.2.cloned.1.call-update) | async-done | bytes 8388624 | tf_op jit(solution)/shard_map/all_gather | solution.py:43
  245.8 0.0 copy-start.2
  245.8 2.0 fusion.22
  247.9 2.3 fusion.20
  250.2 0.0 copy-done
  250.2 1.8 fusion.18
  252.0 1.8 fusion.16
  253.8 0.0 copy-done.2
  253.8 0.6 fusion.14
  254.4 0.6 fusion.12
  255.0 0.6 fusion.10
  255.6 0.0 copy-start.3
  255.6 2.0 copy-done.3
  257.6 1.4 fusion.8
  (2 shorter events, 0.0 us)
Async XLA Ops:
  6.5 127.8 %all-reduce.3.cloned.1.call-start = ((), (), s32[]{:S(2)}) async-start(), calls=%async_computation | async-start | bytes 2097152 | tf_op jit(solution)/shard_map/psum | solution.py:39
  57.3 118.1 %copy-start.1 = (s32[8]{0:T(128)S(1)}, s32[8]{0:T(128)}, u32[]{:S(2)}) copy-start(s32[8]{0:T(128)} %param.7) | copy-start | bytes 100
  57.3 188.5 %all-gather.2.cloned.1.call-start = ((), (), s32[]{:S(2)}) async-start(), calls=%async_computation.1 | async-start | bytes 8912896 | tf_op jit(solution)/shard_map/all_gather | solution.py:43
  175.3 74.9 %copy-start = (bf16[1024,256]{0,1:T(8,128)(2,1)S(1)}, bf16[1024,256]{0,1:T(8,128)(2,1)}, u32[]{:S(2)}) copy-start(bf16[1024,256]{0,1:T(8,128)(2,1)} %multiply_convert_fusion) | copy-start | bytes 1572868
  245.8 8.0 %copy-start.2 = (bf16[1024,4096]{0,1:T(8,128)(2,1)S(1)}, bf16[1024,4096]{0,1:T(8,128)(2,1)}, u32[]{:S(2)}) copy-start(bf16[1024,4096]{0,1:T(8,128)(2,1)} %all-gather.2.cloned.1.call-done) | copy-start | bytes 25165828
  255.6 2.0 copy-start.3
Sparse Core Ops, SparseCore 0:
  57.5 76.8 all-reduce.2
  175.5 70.2 all-gather.1
where the time goes:
time: 267 us; the launch traced here: 266 us
  waiting for transfers between devices  126 us (47%)
  local copies, waits for them, and re-layouts  40 us (15%)
  blocking collectives  37.5 us (14%)
  between operations  34.2 us (13%)
  matrix products  23 us (9%)
  other arithmetic  4.87 us (2%)
    psum x1, waiting for transfers between devices, local(): projected = lax.psum(partial_terms, 'row')  77 us
    all_gather x1, waiting for transfers between devices, local(): every_mode = lax.all_gather(column_modes, 'col', axis=1, tiled=True)  49.1 us
    psum x1, blocking collectives, local(): energy = lax.psum(jnp.sum(projected * projected, axis=1), 'col')  37.5 us
    gather x2, local copies, waits for them, and re-layouts, reorder(): return jnp.take(per_atom, atom_slot, axis=0).reshape(modes_panel.shape)  24 us
    dot_general x1, matrix products, local(): jnp.dot(velocities, panel, preferred_element_type=jnp.float32)  12 us
    dot_general x8, matrix products, correlate(): lax.dot_general(row_modes, shifted, (((0,), (0,)), ((), ())), preferred_e...  11 us
    reshape x1, local copies, waits for them, and re-layouts, reorder(): per_atom = modes_panel.reshape(atom_slot.shape[0], 3, modes_panel.shape[1])  11 us
  transfers between devices with their start and end apart: 2, of which 2 were waited for; matrix products, arithmetic and copies ran while one was open for 0% of the time, Pallas kernels for 0%

commit v1 on v0

v1 whole, which is shorter than its diff:
```python
import jax
import jax.numpy as jnp
from jax import lax
from jax.experimental import pallas as pl
from jax.experimental.pallas import tpu as pltpu
from jax.sharding import PartitionSpec as P

M = 4096
LAGS = 8
MAXLAG = 256
S = 1024
ATOMS = 2560
ROWS = 3 * ATOMS
WIDTH = 256
BLOCK = 128
CHUNKS = 4
UNIT = 16
epsilon = 1e-06

MESH = pl.DeviceIdType.MESH
VMEM = pltpu.VMEM
DMA = pltpu.SemaphoreType.DMA


def project_kernel(
    slot_ref, panel_hbm, v_hbm, row_out, col_out,
    panel, wide, ordered, v_buf, part, landed, energy_send, energy_land, block_t, block_n, moved,
    panel_sem, v_sem, rs_send, rs_recv, e_send, e_recv, c_send, c_recv, t_send, t_recv,
    b_send, b_recv, s_send, s_recv,
):
    r, c = lax.axis_index("row"), lax.axis_index("col")
    y, z = r // 2, r % 2
    chip, core = c // 2, c % 2
    zh, x = chip // 4, chip % 4

    piece = ROWS // CHUNKS
    panel_copies = []
    for i in range(CHUNKS):
        rows = pl.ds(i * piece, piece)
        panel_copies.append(
            pltpu.make_async_copy(panel_hbm.at[rows, :], panel.at[rows, :], panel_sem.at[i])
        )
        panel_copies[-1].start()
    quads = [lax.rem(y + d, 4) for d in (2, 1, 3, 0)]
    v_copies = []
    for i, q in enumerate(quads):
        rows = pl.ds(pl.multiple_of(q * 256, 256), 256)
        v_copies.append(pltpu.make_async_copy(v_hbm.at[rows, :], v_buf.at[i], v_sem.at[i]))
        v_copies[-1].start()

    barrier = pltpu.get_barrier_semaphore()
    for d in range(1, 8):
        pl.semaphore_signal(barrier, inc=1, device_id=(lax.rem(r + d, 8), c), device_id_type=MESH)
    for d in range(1, 16):
        pl.semaphore_signal(barrier, inc=1, device_id=(r, lax.rem(c + d, 16)), device_id_type=MESH)
    partner = (chip, 2 * r + core)
    moves = chip != r

    @pl.when(moves)
    def _():
        pl.semaphore_signal(barrier, inc=1, device_id=partner, device_id_type=MESH)

    for i in range(CHUNKS):
        panel_copies[i].wait()

        def widen(n, _, i=i):
            start = pl.multiple_of(i * piece + n * 64, 64)
            v = panel[pl.ds(start, 64), :].astype(jnp.float32)
            wide[0, pl.ds(8 + start, 64), :] = v[:, :128]
            wide[1, pl.ds(8 + start, 64), :] = v[:, 128:]
            return 0

        lax.fori_loop(0, piece // 64, widen, 0)
    sub = lax.broadcasted_iota(jnp.int32, (8, 128), 0)

    def take(g, _):
        base = [3 * slot_ref[g * UNIT + u] + 8 for u in range(UNIT)]
        for h in range(2):
            tiles = []
            for t in range(3 * UNIT // 8):
                tile = None
                for u in range(UNIT):
                    low = 3 * u - 8 * t
                    if low <= -3 or low >= 8:
                        continue
                    v = wide[h, pl.ds(base[u] - low, 8), :]
                    tile = v if tile is None else jnp.where(sub >= low, v, tile)
                tiles.append(tile)
            for t in range(0, len(tiles), 2):
                both = jnp.concatenate([tiles[t], tiles[t + 1]], axis=0).astype(jnp.bfloat16)
                at = pl.multiple_of(g * (3 * UNIT) + t * 8, 16)
                ordered[pl.ds(at, 16), h * 128 : (h + 1) * 128] = both
        return 0

    lax.fori_loop(0, ATOMS // UNIT, take, 0)

    pl.semaphore_wait(barrier, jnp.where(moves, 23, 22))

    rs_copies = []
    for i, q in enumerate(quads):
        v_copies[i].wait()
        part[i] = jnp.dot(v_buf[i], ordered[...], preferred_element_type=jnp.float32)
        for zz in range(2):
            k = 2 * i + zz
            if k == 7:
                continue
            to_z = lax.rem(z + 1 + zz, 2)
            rows = pl.ds(pl.multiple_of(to_z * BLOCK, BLOCK), BLOCK)
            copy = pltpu.make_async_remote_copy(
                src_ref=part.at[i, rows, :], dst_ref=landed.at[k],
                send_sem=rs_send.at[k], recv_sem=rs_recv.at[k],
                device_id=(2 * q + to_z, c), device_id_type=MESH,
            )
            copy.start()
            rs_copies.append(copy)
    mine = part[3, pl.ds(pl.multiple_of(z * BLOCK, BLOCK), BLOCK), :]
    for k in range(7):
        rs_copies[k].wait_recv()
        mine = mine + landed[k]

    turned = mine.T
    own = jnp.sum(turned * turned, axis=0, keepdims=True)
    energy_send[...] = jnp.broadcast_to(own, (8, BLOCK))
    e_copies = []
    for d in range(1, 16):
        copy = pltpu.make_async_remote_copy(
            src_ref=energy_send, dst_ref=energy_land.at[d - 1],
            send_sem=e_send.at[d - 1], recv_sem=e_recv.at[d - 1],
            device_id=(r, lax.rem(c + d, 16)), device_id_type=MESH,
        )
        copy.start()
        e_copies.append(copy)
    total = own
    for d in range(15):
        e_copies[d].wait_recv()
        total = total + energy_land[d, 0:1, :]
    scaled = turned * lax.rsqrt(total / M + epsilon)
    block_t[...] = scaled.astype(jnp.bfloat16)

    t_copy = pltpu.make_async_remote_copy(
        src_ref=block_t, dst_ref=moved, send_sem=t_send, recv_sem=t_recv,
        device_id=partner, device_id_type=MESH,
    )

    @pl.when(moves)
    def _():
        t_copy.start()

    block_n[...] = scaled.T.astype(jnp.bfloat16)
    own_rows = pl.ds(pl.multiple_of(r * BLOCK, BLOCK), BLOCK)
    c_copies = []
    for d in range(1, 8):
        copy = pltpu.make_async_remote_copy(
            src_ref=block_n, dst_ref=col_out.at[own_rows, :],
            send_sem=c_send.at[d - 1], recv_sem=c_recv.at[d - 1],
            device_id=(lax.rem(r + d, 8), c), device_id_type=MESH,
        )
        copy.start()
        c_copies.append(copy)
    col_out[own_rows, :] = block_n[...]

    @pl.when(moves)
    def _():
        t_copy.wait_recv()

    @pl.when(jnp.logical_not(moves))
    def _():
        moved[...] = block_t[...]

    def place(of_core, of_chip):
        return (
            pl.ds(pl.multiple_of(of_core * WIDTH, WIDTH), WIDTH),
            pl.ds(pl.multiple_of(of_chip * BLOCK, BLOCK), BLOCK),
        )

    here = place(core, chip)
    b_copies = []
    for d in range(1, 8):
        to_chip = lax.rem(zh + d // 4, 2) * 4 + lax.rem(x + d % 4, 4)
        copy = pltpu.make_async_remote_copy(
            src_ref=moved, dst_ref=row_out.at[here],
            send_sem=b_send.at[d - 1], recv_sem=b_recv.at[d - 1],
            device_id=(r, 2 * to_chip + core), device_id_type=MESH,
        )
        copy.start()
        b_copies.append(copy)
    row_out[here] = moved[...]
    other = (r, 2 * chip + 1 - core)
    s_copies = []
    for d in range(8):
        if d:
            b_copies[d - 1].wait_recv()
        from_chip = lax.rem(zh + d // 4, 2) * 4 + lax.rem(x + 4 - d % 4, 4)
        spot = place(core, from_chip)
        copy = pltpu.make_async_remote_copy(
            src_ref=row_out.at[spot] if d else moved, dst_ref=row_out.at[spot],
            send_sem=s_send.at[d], recv_sem=s_recv.at[d],
            device_id=other, device_id_type=MESH,
        )
        copy.start()
        s_copies.append(copy)
    for d in range(8):
        s_copies[d].wait_recv()
    for d in range(7):
        c_copies[d].wait_recv()

    for copy in (*rs_copies, *e_copies, *c_copies, *b_copies, *s_copies):
        copy.wait_send()

    @pl.when(moves)
    def _():
        t_copy.wait_send()


def project(velocities, modes_panel, atom_slot):
    return pl.pallas_call(
        project_kernel,
        out_shape=(
            jax.ShapeDtypeStruct((2 * WIDTH, S), jnp.bfloat16),
            jax.ShapeDtypeStruct((S, WIDTH), jnp.bfloat16),
        ),
        in_specs=[
            pl.BlockSpec(memory_space=pltpu.SMEM),
            pl.BlockSpec(memory_space=pl.ANY),
            pl.BlockSpec(memory_space=pl.ANY),
        ],
        out_specs=(pl.BlockSpec(memory_space=VMEM), pl.BlockSpec(memory_space=VMEM)),
        scratch_shapes=[
            VMEM((ROWS, WIDTH), jnp.bfloat16),
            VMEM((2, ROWS + 16, 128), jnp.float32),
            VMEM((ROWS, WIDTH), jnp.bfloat16),
            VMEM((4, 256, ROWS), jnp.bfloat16),
            VMEM((4, 256, WIDTH), jnp.float32),
            VMEM((7, BLOCK, WIDTH), jnp.float32),
            VMEM((8, BLOCK), jnp.float32),
            VMEM((15, 8, BLOCK), jnp.float32),
            VMEM((WIDTH, BLOCK), jnp.bfloat16),
            VMEM((BLOCK, WIDTH), jnp.bfloat16),
            VMEM((WIDTH, BLOCK), jnp.bfloat16),
            DMA((CHUNKS,)), DMA((4,)),
            DMA((7,)), DMA((7,)),
            DMA((15,)), DMA((15,)),
            DMA((7,)), DMA((7,)),
            DMA, DMA,
            DMA((7,)), DMA((7,)),
            DMA((8,)), DMA((8,)),
        ],
        compiler_params=pltpu.CompilerParams(
            collective_id=0, has_side_effects=True, vmem_limit_bytes=52 * 2**20
        ),
    )(atom_slot, modes_panel, velocities)


def correlate_kernel(lag_ref, rows_ref, cols_ref, out_ref, padded):
    step = pl.program_id(0)

    @pl.when(step == 0)
    def _():
        for h in range(2):
            padded[h, :S, :] = cols_ref[:, h * 128 : (h + 1) * 128].astype(jnp.float32)
            padded[h, S:, :] = jnp.zeros((MAXLAG, 128), jnp.float32)

    lag = lag_ref[step]
    shifted = jnp.concatenate(
        [padded[h, pl.ds(lag, S), :].astype(jnp.bfloat16) for h in range(2)], axis=1
    )
    product = jnp.dot(rows_ref[...], shifted, preferred_element_type=jnp.float32)
    count = jnp.broadcast_to((S - lag).astype(jnp.float32), (1, WIDTH))
    out_ref[0] = product * lax.rsqrt(count)


def correlate(row_modes, column_modes, lag_offsets):
    return pl.pallas_call(
        correlate_kernel,
        grid=(LAGS,),
        out_shape=jax.ShapeDtypeStruct((LAGS, 2 * WIDTH, WIDTH), jnp.float32),
        in_specs=[
            pl.BlockSpec(memory_space=pltpu.SMEM),
            pl.BlockSpec(memory_space=VMEM),
            pl.BlockSpec(memory_space=VMEM),
        ],
        out_specs=pl.BlockSpec((1, 2 * WIDTH, WIDTH), lambda i: (i, 0, 0)),
        scratch_shapes=[VMEM((2, S + MAXLAG, 128), jnp.float32)],
        compiler_params=pltpu.CompilerParams(vmem_limit_bytes=24 * 2**20),
    )(lag_offsets, row_modes, column_modes)


def local(velocities, modes_panel, atom_slot, lag_offsets):
    row_modes, column_modes = project(velocities, modes_panel, atom_slot)
    return correlate(row_modes, column_modes, lag_offsets)


def solution(mesh):
    return jax.shard_map(
        local,
        mesh=mesh,
        in_specs=(P(None, "row"), P("row", "col"), P("row"), P()),
        out_specs=P(None, "row", "col"),
        check_vma=False,
    )
```

time: 267 us -> 63.7 us (0.24)
  waiting for transfers between devices: 126 us -> 0 us
  Pallas kernels: 0 us -> 62.9 us
  local copies, waits for them, and re-layouts: 40 us -> 0.71 us
  blocking collectives: 37.5 us -> 0 us
  between operations: 34.2 us -> 0.02 us
  matrix products: 23 us -> 0 us
  other arithmetic: 4.87 us -> 0 us
    psum x1 -> x0, waiting for transfers between devices: 77 us -> none  [local(): projected = lax.psum(partial_terms, 'row')]
    pallas_call x0 -> x2, Pallas kernels: none -> 62.9 us  [the longest x1 56.7 us: project(): pl.pallas_call(project_kernel, out_shape=(jax.ShapeDtypeStruct((2 * WIDTH...]
    all_gather x1 -> x0, waiting for transfers between devices: 49.1 us -> none  [local(): every_mode = lax.all_gather(column_modes, 'col', axis=1, tiled=True)]
    psum x1 -> x0, blocking collectives: 37.5 us -> none  [local(): energy = lax.psum(jnp.sum(projected * projected, axis=1), 'col')]
    gather x2 -> x0, local copies, waits for them, and re-layouts: 24 us -> none  [reorder(): return jnp.take(per_atom, atom_slot, axis=0).reshape(modes_panel.shape)]
    dot_general x9 -> x0, matrix products: 23 us -> none  [the longest x1 12 us: local(): jnp.dot(velocities, panel, preferred_element_type=jnp.float32)]
    reshape x1 -> x0, local copies, waits for them, and re-layouts: 11 us -> none  [reorder(): per_atom = modes_panel.reshape(atom_slot.shape[0], 3, modes_panel.shape[1])]
  transfers between devices with their start and end apart: 2 -> 0, of which waited for: 2 -> 0; matrix products, arithmetic and copies ran while one was open for 0% -> 0% of each run, Pallas kernels for 0% -> 0%
where the time goes in v1:
time: 63.7 us; the launch traced here: 63.6 us
  Pallas kernels  62.9 us (99%)
  local copies, waits for them, and re-layouts  0.71 us (1%)
    pallas_call x1, Pallas kernels, project(): pl.pallas_call(project_kernel, out_shape=(jax.ShapeDtypeStruct((2 * WIDTH...  56.7 us
    pallas_call x1, Pallas kernels, correlate(): pl.pallas_call(correlate_kernel, grid=(LAGS,), out_shape=jax.ShapeDtypeSt...  6.15 us

profile of v1, /device:TPU:1, one launch (start us, length us, event | category | flops | bytes accessed | tf_op | source)
XLA Modules:
  0.0 63.6 jit_solution(15265021652239981444)
XLA Ops:
  0.0 0.0 copy-start
  0.0 0.7 %copy-done = s32[2560]{0:T(1024)S(1)} copy-done((s32[2560]{0:T(1024)S(1)}, s32[2560]{0:T(1024)}, u32[]{:S(2)}) %copy-start) | copy-done | bytes 10264
  0.7 0.0 copy-start.1
  0.7 56.7 %shard_map.46 = (bf16[512,1024]{1,0:T(8,128)(2,1)S(1)}, bf16[1024,256]{1,0:T(8,128)(2,1)S(1)}) custom-call(s32[2560]{0:T(1024)S(1)} %copy-done, bf16[7680,256]{1,0:T(8,128)(2,1)} %panel_hbm.1, bf16[1024,7680]{1,0:T(8,128)(2,1)} %v_hbm.1), custom_call_target="tpu_custom_call" | custom-call | tf_op jit(solution)/shard_map/pallas_call | solution.py:216
  57.4 0.0 copy-done.1
  57.4 6.2 %shard_map.47 = f32[8,512,256]{2,1,0:T(8,128)} custom-call(s32[8]{0:T(128)S(1)} %copy-done.1, bf16[512,1024]{1,0:T(8,128)(2,1)S(1)} %get-tuple-element.7.rows_ref, bf16[1024,256]{1,0:T(8,128)(2,1)S(1)} %get-tuple-element.8.cols_ref), custom_call_target="tpu_custom_call" | custom-call | tf_op jit(solution)/shard_map/pallas_call | solution.py:273
Async XLA Ops:
  0.0 0.7 %copy-start = (s32[2560]{0:T(1024)S(1)}, s32[2560]{0:T(1024)}, u32[]{:S(2)}) copy-start(s32[2560]{0:T(1024)} %slot_ref.1) | copy-start | bytes 30724
  0.7 56.7 %copy-start.1 = (s32[8]{0:T(128)S(1)}, s32[8]{0:T(128)}, u32[]{:S(2)}) copy-start(s32[8]{0:T(128)} %lag_ref.1) | copy-start | bytes 100

commit v2 on v1

--- a/solution.py
+++ b/solution.py
@@ -23,9 +23,9 @@
 
 
 def project_kernel(
-    slot_ref, panel_hbm, v_hbm, row_out, col_out,
-    panel, wide, ordered, v_buf, part, landed, energy_send, energy_land, block_t, block_n, moved,
-    panel_sem, v_sem, rs_send, rs_recv, e_send, e_recv, c_send, c_recv, t_send, t_recv,
+    slot_hbm, panel_hbm, v_hbm, row_out, col_out,
+    slot_ref, panel, wide, ordered, v_buf, part, landed, energy_send, energy_land, block_t, block_n, moved,
+    slot_sem, panel_sem, v_sem, rs_send, rs_recv, e_send, e_recv, c_send, c_recv, t_send, t_recv,
     b_send, b_recv, s_send, s_recv,
 ):
     r, c = lax.axis_index("row"), lax.axis_index("col")
@@ -33,6 +33,8 @@
     chip, core = c // 2, c % 2
     zh, x = chip // 4, chip % 4
 
+    slot_copy = pltpu.make_async_copy(slot_hbm, slot_ref, slot_sem)
+    slot_copy.start()
     piece = ROWS // CHUNKS
     panel_copies = []
     for i in range(CHUNKS):
@@ -46,7 +48,6 @@
     for i, q in enumerate(quads):
         rows = pl.ds(pl.multiple_of(q * 256, 256), 256)
         v_copies.append(pltpu.make_async_copy(v_hbm.at[rows, :], v_buf.at[i], v_sem.at[i]))
-        v_copies[-1].start()
 
     barrier = pltpu.get_barrier_semaphore()
     for d in range(1, 8):
@@ -62,6 +63,9 @@
 
     for i in range(CHUNKS):
         panel_copies[i].wait()
+        if i == CHUNKS - 1:
+            for copy in v_copies:
+                copy.start()
 
         def widen(n, _, i=i):
             start = pl.multiple_of(i * piece + n * 64, 64)
@@ -71,6 +75,7 @@
             return 0
 
         lax.fori_loop(0, piece // 64, widen, 0)
+    slot_copy.wait()
     sub = lax.broadcasted_iota(jnp.int32, (8, 128), 0)
 
     def take(g, _):
@@ -147,17 +152,45 @@
         t_copy.start()
 
     block_n[...] = scaled.T.astype(jnp.bfloat16)
-    own_rows = pl.ds(pl.multiple_of(r * BLOCK, BLOCK), BLOCK)
-    c_copies = []
-    for d in range(1, 8):
+
+    def rows_of(of_row):
+        return pl.ds(pl.multiple_of(of_row * BLOCK, BLOCK), BLOCK)
+
+    def place(of_chip):
+        return (
+            pl.ds(pl.multiple_of(core * WIDTH, WIDTH), WIDTH),
+            pl.ds(pl.multiple_of(of_chip * BLOCK, BLOCK), BLOCK),
+        )
+
+    def to_row(k, src, rows, device):
         copy = pltpu.make_async_remote_copy(
-            src_ref=block_n, dst_ref=col_out.at[own_rows, :],
-            send_sem=c_send.at[d - 1], recv_sem=c_recv.at[d - 1],
-            device_id=(lax.rem(r + d, 8), c), device_id_type=MESH,
+            src_ref=src, dst_ref=col_out.at[rows, :],
+            send_sem=c_send.at[k], recv_sem=c_recv.at[k],
+            device_id=(device, c), device_id_type=MESH,
         )
         copy.start()
-        c_copies.append(copy)
-    col_out[own_rows, :] = block_n[...]
+        return copy
+
+    def to_col(k, src, spot, chip_to):
+        copy = pltpu.make_async_remote_copy(
+            src_ref=src, dst_ref=row_out.at[spot],
+            send_sem=b_send.at[k], recv_sem=b_recv.at[k],
+            device_id=(r, 2 * chip_to + core), device_id_type=MESH,
+        )
+        copy.start()
+        return copy
+
+    def to_sibling(k, src, spot):
+        copy = pltpu.make_async_remote_copy(
+            src_ref=src, dst_ref=row_out.at[spot],
+            send_sem=s_send.at[k], recv_sem=s_recv.at[k],
+            device_id=(r, 2 * chip + 1 - core), device_id_type=MESH,
+        )
+        copy.start()
+        return copy
+
+    c_copies = [to_row(0, block_n, rows_of(r), 2 * y + 1 - z)]
+    col_out[rows_of(r), :] = block_n[...]
 
     @pl.when(moves)
     def _():
@@ -167,42 +200,31 @@
     def _():
         moved[...] = block_t[...]
 
-    def place(of_core, of_chip):
-        return (
-            pl.ds(pl.multiple_of(of_core * WIDTH, WIDTH), WIDTH),
-            pl.ds(pl.multiple_of(of_chip * BLOCK, BLOCK), BLOCK),
-        )
-
-    here = place(core, chip)
-    b_copies = []
-    for d in range(1, 8):
-        to_chip = lax.rem(zh + d // 4, 2) * 4 + lax.rem(x + d % 4, 4)
-        copy = pltpu.make_async_remote_copy(
-            src_ref=moved, dst_ref=row_out.at[here],
-            send_sem=b_send.at[d - 1], recv_sem=b_recv.at[d - 1],
-            device_id=(r, 2 * to_chip + core), device_id_type=MESH,
-        )
-        copy.start()
-        b_copies.append(copy)
-    row_out[here] = moved[...]
-    other = (r, 2 * chip + 1 - core)
-    s_copies = []
-    for d in range(8):
-        if d:
-            b_copies[d - 1].wait_recv()
-        from_chip = lax.rem(zh + d // 4, 2) * 4 + lax.rem(x + 4 - d % 4, 4)
-        spot = place(core, from_chip)
-        copy = pltpu.make_async_remote_copy(
-            src_ref=row_out.at[spot] if d else moved, dst_ref=row_out.at[spot],
-            send_sem=s_send.at[d], recv_sem=s_recv.at[d],
-            device_id=other, device_id_type=MESH,
-        )
-        copy.start()
-        s_copies.append(copy)
-    for d in range(8):
-        s_copies[d].wait_recv()
-    for d in range(7):
-        c_copies[d].wait_recv()
+    far = 4 * (1 - zh)
+    near = 4 * zh
+    b_copies = [to_col(0, moved, place(chip), far + x)]
+    for d in (2, 1, 3):
+        b_copies.append(to_col(d, moved, place(chip), near + lax.rem(x + d, 4)))
+    for d in (2, 1, 3):
+        c_copies.append(to_row(d, block_n, rows_of(r), 2 * lax.rem(y + d, 4) + z))
+    s_copies = [to_sibling(0, moved, place(chip))]
+    row_out[place(chip)] = moved[...]
+    b_copies[0].wait_recv()
+    other = place(far + x)
+    for d in (2, 1, 3):
+        b_copies.append(to_col(3 + d, row_out.at[other], other, near + lax.rem(x + d, 4)))
+    c_copies[0].wait_recv()
+    beside = rows_of(2 * y + 1 - z)
+    for d in (2, 1, 3):
+        c_copies.append(to_row(3 + d, col_out.at[beside, :], beside, 2 * lax.rem(y + d, 4) + z))
+    s_copies.append(to_sibling(1, row_out.at[other], other))
+    for n, side in enumerate((near, far)):
+        for m, d in enumerate((2, 1, 3)):
+            b_copies[1 + 3 * n + m].wait_recv()
+            spot = place(side + lax.rem(x + 4 - d, 4))
+            s_copies.append(to_sibling(2 + 3 * n + m, row_out.at[spot], spot))
+    for copy in (*s_copies, *c_copies[1:]):
+        copy.wait_recv()
 
     for copy in (*rs_copies, *e_copies, *c_copies, *b_copies, *s_copies):
         copy.wait_send()
@@ -220,12 +242,13 @@
             jax.ShapeDtypeStruct((S, WIDTH), jnp.bfloat16),
         ),
         in_specs=[
-            pl.BlockSpec(memory_space=pltpu.SMEM),
-            pl.BlockSpec(memory_space=pl.ANY),
-            pl.BlockSpec(memory_space=pl.ANY),
+            pl.BlockSpec(memory_space=pltpu.HBM),
+            pl.BlockSpec(memory_space=pltpu.HBM),
+            pl.BlockSpec(memory_space=pltpu.HBM),
         ],
         out_specs=(pl.BlockSpec(memory_space=VMEM), pl.BlockSpec(memory_space=VMEM)),
         scratch_shapes=[
+            pltpu.SMEM((ATOMS,), jnp.int32),
             VMEM((ROWS, WIDTH), jnp.bfloat16),
             VMEM((2, ROWS + 16, 128), jnp.float32),
             VMEM((ROWS, WIDTH), jnp.bfloat16),
@@ -237,7 +260,7 @@
             VMEM((WIDTH, BLOCK), jnp.bfloat16),
             VMEM((BLOCK, WIDTH), jnp.bfloat16),
             VMEM((WIDTH, BLOCK), jnp.bfloat16),
-            DMA((CHUNKS,)), DMA((4,)),
+            DMA, DMA((CHUNKS,)), DMA((4,)),
             DMA((7,)), DMA((7,)),
             DMA((15,)), DMA((15,)),
             DMA((7,)), DMA((7,)),
@@ -251,36 +274,45 @@
     )(atom_slot, modes_panel, velocities)
 
 
-def correlate_kernel(lag_ref, rows_ref, cols_ref, out_ref, padded):
-    step = pl.program_id(0)
-
-    @pl.when(step == 0)
-    def _():
+def correlate_kernel(lag_ref, rows_ref, cols_ref, out_hbm, padded, shifted, held, out_sem):
+    for h in range(2):
+        padded[h, :S, :] = cols_ref[:, h * 128 : (h + 1) * 128].astype(jnp.float32)
+        padded[h, S:, :] = jnp.zeros((MAXLAG, 128), jnp.float32)
+    copies = []
+    for i in range(LAGS):
+        lag = lag_ref[i]
         for h in range(2):
-            padded[h, :S, :] = cols_ref[:, h * 128 : (h + 1) * 128].astype(jnp.float32)
-            padded[h, S:, :] = jnp.zeros((MAXLAG, 128), jnp.float32)
-
-    lag = lag_ref[step]
-    shifted = jnp.concatenate(
-        [padded[h, pl.ds(lag, S), :].astype(jnp.bfloat16) for h in range(2)], axis=1
-    )
-    product = jnp.dot(rows_ref[...], shifted, preferred_element_type=jnp.float32)
-    count = jnp.broadcast_to((S - lag).astype(jnp.float32), (1, WIDTH))
-    out_ref[0] = product * lax.rsqrt(count)
+            cut = padded[h, pl.ds(lag, S), :].astype(jnp.bfloat16)
+            shifted[i % 2, :, h * 128 : (h + 1) * 128] = cut
+        factor = lax.rsqrt(jnp.broadcast_to((S - lag).astype(jnp.float32), (1, WIDTH)))
+        for p in range(2):
+            rows = pl.ds(p * WIDTH, WIDTH)
+            product = jnp.dot(
+                rows_ref[rows, :], shifted[i % 2], preferred_element_type=jnp.float32
+            )
+            held[i, rows, :] = product * factor
+        copies.append(pltpu.make_async_copy(held.at[i], out_hbm.at[i], out_sem.at[i]))
+        copies[-1].start()
+    for copy in copies:
+        copy.wait()
 
 
 def correlate(row_modes, column_modes, lag_offsets):
     return pl.pallas_call(
         correlate_kernel,
-        grid=(LAGS,),
         out_shape=jax.ShapeDtypeStruct((LAGS, 2 * WIDTH, WIDTH), jnp.float32),
         in_specs=[
             pl.BlockSpec(memory_space=pltpu.SMEM),
             pl.BlockSpec(memory_space=VMEM),
             pl.BlockSpec(memory_space=VMEM),
         ],
-        out_specs=pl.BlockSpec((1, 2 * WIDTH, WIDTH), lambda i: (i, 0, 0)),
-        scratch_shapes=[VMEM((2, S + MAXLAG, 128), jnp.float32)],
+        out_specs=pl.BlockSpec(memory_space=pl.ANY),
+        scratch_shapes=[
+            VMEM((2, S + MAXLAG, 128), jnp.float32),
+            VMEM((2, S, WIDTH), jnp.bfloat16),
+            VMEM((LAGS, 2 * WIDTH, WIDTH), jnp.float32),
+            DMA((LAGS,)),
+        ],
         compiler_params=pltpu.CompilerParams(vmem_limit_bytes=24 * 2**20),
     )(lag_offsets, row_modes, column_modes)
 

time: 63.7 us -> 57.5 us (0.903)
  Pallas kernels: 62.9 us -> 56.6 us
    pallas_call x1, Pallas kernels: 56.7 us -> 52.4 us  [project(): pl.pallas_call(project_kernel, out_shape=(jax.ShapeDtypeStruct((2 * WIDTH...]
    pallas_call x1, Pallas kernels: 6.15 us -> 4.24 us  [correlate(): pl.pallas_call(correlate_kernel, out_shape=jax.ShapeDtypeStruct((LAGS, 2...]
where the time goes in v2:
time: 57.5 us; the launch traced here: 57.3 us
  Pallas kernels  56.6 us (98%)
  local copies, waits for them, and re-layouts  0.71 us (1%)
    pallas_call x1, Pallas kernels, project(): pl.pallas_call(project_kernel, out_shape=(jax.ShapeDtypeStruct((2 * WIDTH...  52.4 us
    pallas_call x1, Pallas kernels, correlate(): pl.pallas_call(correlate_kernel, out_shape=jax.ShapeDtypeStruct((LAGS, 2...  4.24 us

profile of v2, /device:TPU:1, one launch (start us, length us, event | category | flops | bytes accessed | tf_op | source)
XLA Modules:
  0.0 57.3 jit_solution(3365970177360437363)
XLA Ops:
  0.0 0.0 copy-start
  0.0 0.7 %copy-done = s32[2560]{0:T(1024)S(1)} copy-done((s32[2560]{0:T(1024)S(1)}, s32[2560]{0:T(1024)}, u32[]{:S(2)}) %copy-start) | copy-done | bytes 10264
  0.7 0.0 copy-start.1
  0.7 52.4 %shard_map.46 = (bf16[512,1024]{1,0:T(8,128)(2,1)S(1)}, bf16[1024,256]{1,0:T(8,128)(2,1)S(1)}) custom-call(s32[2560]{0:T(1024)S(1)} %copy-done, bf16[7680,256]{1,0:T(8,128)(2,1)} %panel_hbm.1, bf16[1024,7680]{1,0:T(8,128)(2,1)} %v_hbm.1), custom_call_target="tpu_custom_call" | custom-call | tf_op jit(solution)/shard_map/pallas_call | solution.py:238
  53.1 0.0 copy-done.1
  53.1 4.2 %shard_map.47 = f32[8,512,256]{2,1,0:T(8,128)} custom-call(s32[8]{0:T(128)S(1)} %copy-done.1, bf16[512,1024]{1,0:T(8,128)(2,1)S(1)} %get-tuple-element.7.rows_ref, bf16[1024,256]{1,0:T(8,128)(2,1)S(1)} %get-tuple-element.8.cols_ref), custom_call_target="tpu_custom_call" | custom-call | tf_op jit(solution)/shard_map/pallas_call | solution.py:301
Async XLA Ops:
  0.0 0.7 %copy-start = (s32[2560]{0:T(1024)S(1)}, s32[2560]{0:T(1024)}, u32[]{:S(2)}) copy-start(s32[2560]{0:T(1024)} %slot_hbm.1) | copy-start | bytes 30724
  0.7 52.4 %copy-start.1 = (s32[8]{0:T(128)S(1)}, s32[8]{0:T(128)}, u32[]{:S(2)}) copy-start(s32[8]{0:T(128)} %lag_ref.1) | copy-start | bytes 100

commit v3 on v2

--- a/solution.py
+++ b/solution.py
@@ -15,6 +15,7 @@
 BLOCK = 128
 CHUNKS = 4
 UNIT = 16
+TINY = 1e-30
 epsilon = 1e-06
 
 MESH = pl.DeviceIdType.MESH
@@ -24,7 +25,7 @@
 
 def project_kernel(
     slot_hbm, panel_hbm, v_hbm, row_out, col_out,
-    slot_ref, panel, wide, ordered, v_buf, part, landed, energy_send, energy_land, block_t, block_n, moved,
+    slot_ref, panel, wide, ordered, v_buf, sent, landed, energy_send, energy_land, block_t, block_n, moved,
     slot_sem, panel_sem, v_sem, rs_send, rs_recv, e_send, e_recv, c_send, c_recv, t_send, t_recv,
     b_send, b_recv, s_send, s_recv,
 ):
@@ -102,28 +103,41 @@
     pl.semaphore_wait(barrier, jnp.where(moves, 23, 22))
 
     rs_copies = []
+    mine = None
     for i, q in enumerate(quads):
         v_copies[i].wait()
-        part[i] = jnp.dot(v_buf[i], ordered[...], preferred_element_type=jnp.float32)
+        part = jnp.dot(v_buf[i], ordered[...], preferred_element_type=jnp.float32)
+        part = part.T
+        top = jnp.max(jnp.abs(part), axis=0, keepdims=True)
+        power = jnp.ceil(jnp.log2(jnp.maximum(top, TINY)))
+        coded = jnp.clip(jnp.round(part * jnp.exp2(15.0 - power)), -32767.0, 32767.0)
+        coded = coded.astype(jnp.int32).astype(jnp.int16)
+        powers = jnp.broadcast_to(power, (16, 2 * BLOCK)).astype(jnp.int32).astype(jnp.int16)
+        for zz in range(2):
+            half = slice(zz * BLOCK, (zz + 1) * BLOCK)
+            sent[i, zz, :WIDTH, :] = coded[:, half]
+            sent[i, zz, WIDTH:, :] = powers[:, half]
+        if i == 3:
+            mine = jnp.where(z == 0, part[:, :BLOCK], part[:, BLOCK:])
         for zz in range(2):
             k = 2 * i + zz
             if k == 7:
                 continue
             to_z = lax.rem(z + 1 + zz, 2)
-            rows = pl.ds(pl.multiple_of(to_z * BLOCK, BLOCK), BLOCK)
             copy = pltpu.make_async_remote_copy(
-                src_ref=part.at[i, rows, :], dst_ref=landed.at[k],
+                src_ref=sent.at[i, to_z], dst_ref=landed.at[k],
                 send_sem=rs_send.at[k], recv_sem=rs_recv.at[k],
                 device_id=(2 * q + to_z, c), device_id_type=MESH,
             )
             copy.start()
             rs_copies.append(copy)
-    mine = part[3, pl.ds(pl.multiple_of(z * BLOCK, BLOCK), BLOCK), :]
+    turned = mine
     for k in range(7):
         rs_copies[k].wait_recv()
-        mine = mine + landed[k]
-
-    turned = mine.T
+        power = landed[k, WIDTH:, :].astype(jnp.int32).astype(jnp.float32)[0:1, :]
+        value = landed[k, :WIDTH, :].astype(jnp.int32).astype(jnp.float32)
+        turned = turned + value * jnp.exp2(power - 15.0)
+
     own = jnp.sum(turned * turned, axis=0, keepdims=True)
     energy_send[...] = jnp.broadcast_to(own, (8, BLOCK))
     e_copies = []
@@ -253,8 +267,8 @@
             VMEM((2, ROWS + 16, 128), jnp.float32),
             VMEM((ROWS, WIDTH), jnp.bfloat16),
             VMEM((4, 256, ROWS), jnp.bfloat16),
-            VMEM((4, 256, WIDTH), jnp.float32),
-            VMEM((7, BLOCK, WIDTH), jnp.float32),
+            VMEM((4, 2, WIDTH + 16, BLOCK), jnp.int16),
+            VMEM((7, WIDTH + 16, BLOCK), jnp.int16),
             VMEM((8, BLOCK), jnp.float32),
             VMEM((15, 8, BLOCK), jnp.float32),
             VMEM((WIDTH, BLOCK), jnp.bfloat16),

time: 57.5 us -> 52.5 us (0.913)
  Pallas kernels: 56.6 us -> 51.6 us
    pallas_call x1, Pallas kernels: 52.4 us -> 47.4 us  [project(): pl.pallas_call(project_kernel, out_shape=(jax.ShapeDtypeStruct((2 * WIDTH...]
where the time goes in v3:
time: 52.5 us; the launch traced here: 52.4 us
  Pallas kernels  51.6 us (98%)
  local copies, waits for them, and re-layouts  0.71 us (1%)
    pallas_call x1, Pallas kernels, project(): pl.pallas_call(project_kernel, out_shape=(jax.ShapeDtypeStruct((2 * WIDTH...  47.4 us
    pallas_call x1, Pallas kernels, correlate(): pl.pallas_call(correlate_kernel, out_shape=jax.ShapeDtypeStruct((LAGS, 2...  4.24 us

profile of v3, /device:TPU:1, one launch (start us, length us, event | category | flops | bytes accessed | tf_op | source)
XLA Modules:
  0.0 52.4 jit_solution(4089377468569902307)
XLA Ops:
  0.0 0.0 copy-start
  0.0 0.7 %copy-done = s32[2560]{0:T(1024)S(1)} copy-done((s32[2560]{0:T(1024)S(1)}, s32[2560]{0:T(1024)}, u32[]{:S(2)}) %copy-start) | copy-done | bytes 10264
  0.7 0.0 copy-start.1
  0.7 47.4 %shard_map.46 = (bf16[512,1024]{1,0:T(8,128)(2,1)S(1)}, bf16[1024,256]{1,0:T(8,128)(2,1)S(1)}) custom-call(s32[2560]{0:T(1024)S(1)} %copy-done, bf16[7680,256]{1,0:T(8,128)(2,1)} %panel_hbm.1, bf16[1024,7680]{1,0:T(8,128)(2,1)} %v_hbm.1), custom_call_target="tpu_custom_call" | custom-call | tf_op jit(solution)/shard_map/pallas_call | solution.py:252
  48.1 0.0 copy-done.1
  48.1 4.2 %shard_map.47 = f32[8,512,256]{2,1,0:T(8,128)} custom-call(s32[8]{0:T(128)S(1)} %copy-done.1, bf16[512,1024]{1,0:T(8,128)(2,1)S(1)} %get-tuple-element.7.rows_ref, bf16[1024,256]{1,0:T(8,128)(2,1)S(1)} %get-tuple-element.8.cols_ref), custom_call_target="tpu_custom_call" | custom-call | tf_op jit(solution)/shard_map/pallas_call | solution.py:315
Async XLA Ops:
  0.0 0.7 %copy-start = (s32[2560]{0:T(1024)S(1)}, s32[2560]{0:T(1024)}, u32[]{:S(2)}) copy-start(s32[2560]{0:T(1024)} %slot_hbm.1) | copy-start | bytes 30724
  0.7 47.4 %copy-start.1 = (s32[8]{0:T(128)S(1)}, s32[8]{0:T(128)}, u32[]{:S(2)}) copy-start(s32[8]{0:T(128)} %lag_ref.1) | copy-start | bytes 100

commit v4 on v3

--- a/solution.py
+++ b/solution.py
@@ -23,10 +23,23 @@
 DMA = pltpu.SemaphoreType.DMA
 
 
+def code(values):
+    top = jnp.max(jnp.abs(values), axis=0, keepdims=True)
+    power = jnp.ceil(jnp.log2(jnp.maximum(top, TINY)))
+    coded = jnp.clip(jnp.round(values * jnp.exp2(15.0 - power)), -32767.0, 32767.0)
+    powers = jnp.broadcast_to(power, (16, values.shape[1]))
+    return coded.astype(jnp.int32).astype(jnp.int16), powers.astype(jnp.int32).astype(jnp.int16)
+
+
+def decode(ref):
+    power = ref[WIDTH:, :].astype(jnp.int32).astype(jnp.float32)[0:1, :]
+    return ref[:WIDTH, :].astype(jnp.int32).astype(jnp.float32) * jnp.exp2(power - 15.0)
+
+
 def project_kernel(
     slot_hbm, panel_hbm, v_hbm, row_out, col_out,
-    slot_ref, panel, wide, ordered, v_buf, sent, landed, energy_send, energy_land, block_t, block_n, moved,
-    slot_sem, panel_sem, v_sem, rs_send, rs_recv, e_send, e_recv, c_send, c_recv, t_send, t_recv,
+    slot_ref, panel, wide, ordered, v_buf, sent, landed, energy_send, energy_land, there_land, t_sent, t_land, block_n, moved,
+    slot_sem, panel_sem, v_sem, rs_send, rs_recv, e_send, e_recv, there_send, there_recv, c_send, c_recv, t_send, t_recv,
     b_send, b_recv, s_send, s_recv,
 ):
     r, c = lax.axis_index("row"), lax.axis_index("col")
@@ -60,7 +73,8 @@
 
     @pl.when(moves)
     def _():
-        pl.semaphore_signal(barrier, inc=1, device_id=partner, device_id_type=MESH)
+        for k in range(16):
+            pl.semaphore_signal(barrier, inc=1, device_id=(chip, k), device_id_type=MESH)
 
     for i in range(CHUNKS):
         panel_copies[i].wait()
@@ -100,7 +114,7 @@
 
     lax.fori_loop(0, ATOMS // UNIT, take, 0)
 
-    pl.semaphore_wait(barrier, jnp.where(moves, 23, 22))
+    pl.semaphore_wait(barrier, 36)
 
     rs_copies = []
     mine = None
@@ -108,11 +122,7 @@
         v_copies[i].wait()
         part = jnp.dot(v_buf[i], ordered[...], preferred_element_type=jnp.float32)
         part = part.T
-        top = jnp.max(jnp.abs(part), axis=0, keepdims=True)
-        power = jnp.ceil(jnp.log2(jnp.maximum(top, TINY)))
-        coded = jnp.clip(jnp.round(part * jnp.exp2(15.0 - power)), -32767.0, 32767.0)
-        coded = coded.astype(jnp.int32).astype(jnp.int16)
-        powers = jnp.broadcast_to(power, (16, 2 * BLOCK)).astype(jnp.int32).astype(jnp.int16)
+        coded, powers = code(part)
         for zz in range(2):
             half = slice(zz * BLOCK, (zz + 1) * BLOCK)
             sent[i, zz, :WIDTH, :] = coded[:, half]
@@ -134,13 +144,32 @@
     turned = mine
     for k in range(7):
         rs_copies[k].wait_recv()
-        power = landed[k, WIDTH:, :].astype(jnp.int32).astype(jnp.float32)[0:1, :]
-        value = landed[k, :WIDTH, :].astype(jnp.int32).astype(jnp.float32)
-        turned = turned + value * jnp.exp2(power - 15.0)
+        turned = turned + decode(landed.at[k])
+
+    t_sent[:WIDTH, :], t_sent[WIDTH:, :] = code(turned)
+    t_copy = pltpu.make_async_remote_copy(
+        src_ref=t_sent, dst_ref=t_land, send_sem=t_send, recv_sem=t_recv,
+        device_id=partner, device_id_type=MESH,
+    )
+
+    @pl.when(moves)
+    def _():
+        t_copy.start()
 
     own = jnp.sum(turned * turned, axis=0, keepdims=True)
     energy_send[...] = jnp.broadcast_to(own, (8, BLOCK))
     e_copies = []
+    for d in range(1, 8):
+        for k in range(2):
+            n = 2 * (d - 1) + k
+            copy = pltpu.make_async_remote_copy(
+                src_ref=energy_send, dst_ref=there_land.at[c],
+                send_sem=there_send.at[n], recv_sem=there_recv.at[c],
+                device_id=(lax.rem(r + d, 8), 2 * r + k), device_id_type=MESH,
+            )
+            copy.start()
+            e_copies.append(copy)
+    own_copies = []
     for d in range(1, 16):
         copy = pltpu.make_async_remote_copy(
             src_ref=energy_send, dst_ref=energy_land.at[d - 1],
@@ -148,23 +177,13 @@
             device_id=(r, lax.rem(c + d, 16)), device_id_type=MESH,
         )
         copy.start()
-        e_copies.append(copy)
+        own_copies.append(copy)
+    e_copies += own_copies
     total = own
     for d in range(15):
-        e_copies[d].wait_recv()
+        own_copies[d].wait_recv()
         total = total + energy_land[d, 0:1, :]
     scaled = turned * lax.rsqrt(total / M + epsilon)
-    block_t[...] = scaled.astype(jnp.bfloat16)
-
-    t_copy = pltpu.make_async_remote_copy(
-        src_ref=block_t, dst_ref=moved, send_sem=t_send, recv_sem=t_recv,
-        device_id=partner, device_id_type=MESH,
-    )
-
-    @pl.when(moves)
-    def _():
-        t_copy.start()
-
     block_n[...] = scaled.T.astype(jnp.bfloat16)
 
     def rows_of(of_row):
@@ -208,11 +227,20 @@
 
     @pl.when(moves)
     def _():
+        energy = jnp.zeros((1, BLOCK), jnp.float32)
+        for k in range(16):
+            pltpu.make_async_remote_copy(
+                src_ref=energy_send, dst_ref=there_land.at[k],
+                send_sem=there_send.at[0], recv_sem=there_recv.at[k],
+                device_id=partner, device_id_type=MESH,
+            ).wait_recv()
+            energy = energy + there_land[k, 0:1, :]
         t_copy.wait_recv()
+        moved[...] = (decode(t_land) * lax.rsqrt(energy / M + epsilon)).astype(jnp.bfloat16)
 
     @pl.when(jnp.logical_not(moves))
     def _():
-        moved[...] = block_t[...]
+        moved[...] = scaled.astype(jnp.bfloat16)
 
     far = 4 * (1 - zh)
     near = 4 * zh
@@ -271,12 +299,15 @@
             VMEM((7, WIDTH + 16, BLOCK), jnp.int16),
             VMEM((8, BLOCK), jnp.float32),
             VMEM((15, 8, BLOCK), jnp.float32),
-            VMEM((WIDTH, BLOCK), jnp.bfloat16),
+            VMEM((16, 8, BLOCK), jnp.float32),
+            VMEM((WIDTH + 16, BLOCK), jnp.int16),
+            VMEM((WIDTH + 16, BLOCK), jnp.int16),
             VMEM((BLOCK, WIDTH), jnp.bfloat16),
             VMEM((WIDTH, BLOCK), jnp.bfloat16),
             DMA, DMA((CHUNKS,)), DMA((4,)),
             DMA((7,)), DMA((7,)),
             DMA((15,)), DMA((15,)),
+            DMA((14,)), DMA((16,)),
             DMA((7,)), DMA((7,)),
             DMA, DMA,
             DMA((7,)), DMA((7,)),

time: 52.5 us -> 50.4 us (0.960)
  Pallas kernels: 51.6 us -> 49.5 us
    pallas_call x1, Pallas kernels: 47.4 us -> 45.3 us  [project(): pl.pallas_call(project_kernel, out_shape=(jax.ShapeDtypeStruct((2 * WIDTH...]
where the time goes in v4:
time: 50.4 us; the launch traced here: 50.3 us
  Pallas kernels  49.5 us (98%)
  local copies, waits for them, and re-layouts  0.71 us (1%)
    pallas_call x1, Pallas kernels, project(): pl.pallas_call(project_kernel, out_shape=(jax.ShapeDtypeStruct((2 * WIDTH...  45.3 us
    pallas_call x1, Pallas kernels, correlate(): pl.pallas_call(correlate_kernel, out_shape=jax.ShapeDtypeStruct((LAGS, 2...  4.26 us

profile of v4, /device:TPU:1, one launch (start us, length us, event | category | flops | bytes accessed | tf_op | source)
XLA Modules:
  0.0 50.3 jit_solution(10380248641154163588)
XLA Ops:
  0.0 0.0 copy-start
  0.0 0.7 %copy-done = s32[2560]{0:T(1024)S(1)} copy-done((s32[2560]{0:T(1024)S(1)}, s32[2560]{0:T(1024)}, u32[]{:S(2)}) %copy-start) | copy-done | bytes 10264
  0.7 0.0 copy-start.1
  0.7 45.3 %shard_map.46 = (bf16[512,1024]{1,0:T(8,128)(2,1)S(1)}, bf16[1024,256]{1,0:T(8,128)(2,1)S(1)}) custom-call(s32[2560]{0:T(1024)S(1)} %copy-done, bf16[7680,256]{1,0:T(8,128)(2,1)} %panel_hbm.1, bf16[1024,7680]{1,0:T(8,128)(2,1)} %v_hbm.1), custom_call_target="tpu_custom_call" | custom-call | tf_op jit(solution)/shard_map/pallas_call | solution.py:280
  46.0 0.0 copy-done.1
  46.0 4.3 %shard_map.47 = f32[8,512,256]{2,1,0:T(8,128)} custom-call(s32[8]{0:T(128)S(1)} %copy-done.1, bf16[512,1024]{1,0:T(8,128)(2,1)S(1)} %get-tuple-element.7.rows_ref, bf16[1024,256]{1,0:T(8,128)(2,1)S(1)} %get-tuple-element.8.cols_ref), custom_call_target="tpu_custom_call" | custom-call | tf_op jit(solution)/shard_map/pallas_call | solution.py:346
Async XLA Ops:
  0.0 0.7 %copy-start = (s32[2560]{0:T(1024)S(1)}, s32[2560]{0:T(1024)}, u32[]{:S(2)}) copy-start(s32[2560]{0:T(1024)} %slot_hbm.1) | copy-start | bytes 30724
  0.7 45.3 %copy-start.1 = (s32[8]{0:T(128)S(1)}, s32[8]{0:T(128)}, u32[]{:S(2)}) copy-start(s32[8]{0:T(128)} %lag_ref.1) | copy-start | bytes 100

commit v5 on v4

--- a/solution.py
+++ b/solution.py
@@ -16,6 +16,7 @@
 CHUNKS = 4
 UNIT = 16
 TINY = 1e-30
+FULL = 32760.0
 epsilon = 1e-06
 
 MESH = pl.DeviceIdType.MESH
@@ -26,19 +27,19 @@
 def code(values):
     top = jnp.max(jnp.abs(values), axis=0, keepdims=True)
     power = jnp.ceil(jnp.log2(jnp.maximum(top, TINY)))
-    coded = jnp.clip(jnp.round(values * jnp.exp2(15.0 - power)), -32767.0, 32767.0)
+    coded = jnp.round(values * (FULL * jnp.exp2(-power)))
     powers = jnp.broadcast_to(power, (16, values.shape[1]))
     return coded.astype(jnp.int32).astype(jnp.int16), powers.astype(jnp.int32).astype(jnp.int16)
 
 
 def decode(ref):
     power = ref[WIDTH:, :].astype(jnp.int32).astype(jnp.float32)[0:1, :]
-    return ref[:WIDTH, :].astype(jnp.int32).astype(jnp.float32) * jnp.exp2(power - 15.0)
+    return ref[:WIDTH, :].astype(jnp.int32).astype(jnp.float32) * (jnp.exp2(power) / FULL)
 
 
 def project_kernel(
     slot_hbm, panel_hbm, v_hbm, row_out, col_out,
-    slot_ref, panel, wide, ordered, v_buf, sent, landed, energy_send, energy_land, there_land, t_sent, t_land, block_n, moved,
+    slot_ref, panel, wide, ordered, v_buf, part, sent, landed, energy_send, energy_land, there_land, t_sent, t_land, block_n, moved,
     slot_sem, panel_sem, v_sem, rs_send, rs_recv, e_send, e_recv, there_send, there_recv, c_send, c_recv, t_send, t_recv,
     b_send, b_recv, s_send, s_recv,
 ):
@@ -57,7 +58,7 @@
             pltpu.make_async_copy(panel_hbm.at[rows, :], panel.at[rows, :], panel_sem.at[i])
         )
         panel_copies[-1].start()
-    quads = [lax.rem(y + d, 4) for d in (2, 1, 3, 0)]
+    quads = [lax.rem(y + i + 1, 4) for i in range(4)]
     v_copies = []
     for i, q in enumerate(quads):
         rows = pl.ds(pl.multiple_of(q * 256, 256), 256)
@@ -116,32 +117,33 @@
 
     pl.semaphore_wait(barrier, 36)
 
-    rs_copies = []
-    mine = None
-    for i, q in enumerate(quads):
-        v_copies[i].wait()
-        part = jnp.dot(v_buf[i], ordered[...], preferred_element_type=jnp.float32)
-        part = part.T
-        coded, powers = code(part)
+    def rs_copy(i, zz):
+        to_z = lax.rem(z + 1 + zz, 2)
+        k = 2 * i + zz
+        return pltpu.make_async_remote_copy(
+            src_ref=sent.at[i, to_z], dst_ref=landed.at[k],
+            send_sem=rs_send.at[k], recv_sem=rs_recv.at[k],
+            device_id=(2 * lax.rem(y + i + 1, 4) + to_z, c), device_id_type=MESH,
+        )
+
+    def step(i, _):
+        pltpu.make_async_copy(v_hbm.at[pl.ds(0, 256), :], v_buf.at[i], v_sem.at[i]).wait()
+        part[i] = jnp.dot(v_buf[i], ordered[...], preferred_element_type=jnp.float32)
         for zz in range(2):
-            half = slice(zz * BLOCK, (zz + 1) * BLOCK)
-            sent[i, zz, :WIDTH, :] = coded[:, half]
-            sent[i, zz, WIDTH:, :] = powers[:, half]
-        if i == 3:
-            mine = jnp.where(z == 0, part[:, :BLOCK], part[:, BLOCK:])
-        for zz in range(2):
-            k = 2 * i + zz
-            if k == 7:
-                continue
-            to_z = lax.rem(z + 1 + zz, 2)
-            copy = pltpu.make_async_remote_copy(
-                src_ref=sent.at[i, to_z], dst_ref=landed.at[k],
-                send_sem=rs_send.at[k], recv_sem=rs_recv.at[k],
-                device_id=(2 * q + to_z, c), device_id_type=MESH,
-            )
-            copy.start()
-            rs_copies.append(copy)
-    turned = mine
+            coded, powers = code(part[i, zz * BLOCK : (zz + 1) * BLOCK, :].T)
+            sent[i, zz, :WIDTH, :] = coded
+            sent[i, zz, WIDTH:, :] = powers
+        rs_copy(i, 0).start()
+
+        @pl.when(i < 3)
+        def _():
+            rs_copy(i, 1).start()
+
+        return 0
+
+    lax.fori_loop(0, 4, step, 0)
+    rs_copies = [rs_copy(k // 2, k % 2) for k in range(7)]
+    turned = part[3, pl.ds(pl.multiple_of(z * BLOCK, BLOCK), BLOCK), :].T
     for k in range(7):
         rs_copies[k].wait_recv()
         turned = turned + decode(landed.at[k])
@@ -295,6 +297,7 @@
             VMEM((2, ROWS + 16, 128), jnp.float32),
             VMEM((ROWS, WIDTH), jnp.bfloat16),
             VMEM((4, 256, ROWS), jnp.bfloat16),
+            VMEM((4, 2 * BLOCK, WIDTH), jnp.float32),
             VMEM((4, 2, WIDTH + 16, BLOCK), jnp.int16),
             VMEM((7, WIDTH + 16, BLOCK), jnp.int16),
             VMEM((8, BLOCK), jnp.float32),

time: 50.4 us -> 48 us (0.952)
  Pallas kernels: 49.5 us -> 46.9 us
    pallas_call x1, Pallas kernels: 45.3 us -> 42.7 us  [project(): pl.pallas_call(project_kernel, out_shape=(jax.ShapeDtypeStruct((2 * WIDTH...]
where the time goes in v5:
time: 48 us; the launch traced here: 47.6 us
  Pallas kernels  46.9 us (98%)
  local copies, waits for them, and re-layouts  0.71 us (1%)
    pallas_call x1, Pallas kernels, project(): pl.pallas_call(project_kernel, out_shape=(jax.ShapeDtypeStruct((2 * WIDTH...  42.7 us
    pallas_call x1, Pallas kernels, correlate(): pl.pallas_call(correlate_kernel, out_shape=jax.ShapeDtypeStruct((LAGS, 2...  4.25 us

profile of v5, /device:TPU:1, one launch (start us, length us, event | category | flops | bytes accessed | tf_op | source)
XLA Modules:
  0.0 47.6 jit_solution(15044301077637595940)
XLA Ops:
  0.0 0.0 copy-start
  0.0 0.7 %copy-done = s32[2560]{0:T(1024)S(1)} copy-done((s32[2560]{0:T(1024)S(1)}, s32[2560]{0:T(1024)}, u32[]{:S(2)}) %copy-start) | copy-done | bytes 10264
  0.7 0.0 copy-start.1
  0.7 42.7 %shard_map.46 = (bf16[512,1024]{1,0:T(8,128)(2,1)S(1)}, bf16[1024,256]{1,0:T(8,128)(2,1)S(1)}) custom-call(s32[2560]{0:T(1024)S(1)} %copy-done, bf16[7680,256]{1,0:T(8,128)(2,1)} %panel_hbm.1, bf16[1024,7680]{1,0:T(8,128)(2,1)} %v_hbm.1), custom_call_target="tpu_custom_call" | custom-call | tf_op jit(solution)/shard_map/pallas_call | solution.py:282
  43.4 0.0 copy-done.1
  43.4 4.2 %shard_map.47 = f32[8,512,256]{2,1,0:T(8,128)} custom-call(s32[8]{0:T(128)S(1)} %copy-done.1, bf16[512,1024]{1,0:T(8,128)(2,1)S(1)} %get-tuple-element.7.rows_ref, bf16[1024,256]{1,0:T(8,128)(2,1)S(1)} %get-tuple-element.8.cols_ref), custom_call_target="tpu_custom_call" | custom-call | tf_op jit(solution)/shard_map/pallas_call | solution.py:349
Async XLA Ops:
  0.0 0.7 %copy-start = (s32[2560]{0:T(1024)S(1)}, s32[2560]{0:T(1024)}, u32[]{:S(2)}) copy-start(s32[2560]{0:T(1024)} %slot_hbm.1) | copy-start | bytes 30724
  0.7 42.7 %copy-start.1 = (s32[8]{0:T(128)S(1)}, s32[8]{0:T(128)}, u32[]{:S(2)}) copy-start(s32[8]{0:T(128)} %lag_ref.1) | copy-start | bytes 100

commit v6 on v5

--- a/solution.py
+++ b/solution.py
@@ -39,7 +39,7 @@
 
 def project_kernel(
     slot_hbm, panel_hbm, v_hbm, row_out, col_out,
-    slot_ref, panel, wide, ordered, v_buf, part, sent, landed, energy_send, energy_land, there_land, t_sent, t_land, block_n, moved,
+    slot_ref, panel, wide, ordered, v_buf, part, sent, landed, energy_send, energy_land, there_land, there_sum, t_sent, t_land, block_n, moved,
     slot_sem, panel_sem, v_sem, rs_send, rs_recv, e_send, e_recv, there_send, there_recv, c_send, c_recv, t_send, t_recv,
     b_send, b_recv, s_send, s_recv,
 ):
@@ -69,13 +69,15 @@
         pl.semaphore_signal(barrier, inc=1, device_id=(lax.rem(r + d, 8), c), device_id_type=MESH)
     for d in range(1, 16):
         pl.semaphore_signal(barrier, inc=1, device_id=(r, lax.rem(c + d, 16)), device_id_type=MESH)
-    partner = (chip, 2 * r + core)
-    moves = chip != r
-
-    @pl.when(moves)
+    target = (chip, 2 * lax.rem(r + chip, 8) + core)
+    origin = lax.rem(chip + 8 - r, 8)
+    moves = (r != 0) | (chip != 0)
+    elsewhere = origin != r
+
+    @pl.when(elsewhere)
     def _():
         for k in range(16):
-            pl.semaphore_signal(barrier, inc=1, device_id=(chip, k), device_id_type=MESH)
+            pl.semaphore_signal(barrier, inc=1, device_id=(origin, k), device_id_type=MESH)
 
     for i in range(CHUNKS):
         panel_copies[i].wait()
@@ -151,7 +153,7 @@
     t_sent[:WIDTH, :], t_sent[WIDTH:, :] = code(turned)
     t_copy = pltpu.make_async_remote_copy(
         src_ref=t_sent, dst_ref=t_land, send_sem=t_send, recv_sem=t_recv,
-        device_id=partner, device_id_type=MESH,
+        device_id=target, device_id_type=MESH,
     )
 
     @pl.when(moves)
@@ -162,12 +164,13 @@
     energy_send[...] = jnp.broadcast_to(own, (8, BLOCK))
     e_copies = []
     for d in range(1, 8):
+        to_row_of = lax.rem(r + d, 8)
         for k in range(2):
             n = 2 * (d - 1) + k
             copy = pltpu.make_async_remote_copy(
                 src_ref=energy_send, dst_ref=there_land.at[c],
                 send_sem=there_send.at[n], recv_sem=there_recv.at[c],
-                device_id=(lax.rem(r + d, 8), 2 * r + k), device_id_type=MESH,
+                device_id=(to_row_of, 2 * lax.rem(to_row_of + r, 8) + k), device_id_type=MESH,
             )
             copy.start()
             e_copies.append(copy)
@@ -192,9 +195,10 @@
         return pl.ds(pl.multiple_of(of_row * BLOCK, BLOCK), BLOCK)
 
     def place(of_chip):
+        of_row = lax.rem(of_chip + 8 - r, 8)
         return (
             pl.ds(pl.multiple_of(core * WIDTH, WIDTH), WIDTH),
-            pl.ds(pl.multiple_of(of_chip * BLOCK, BLOCK), BLOCK),
+            pl.ds(pl.multiple_of(of_row * BLOCK, BLOCK), BLOCK),
         )
 
     def to_row(k, src, rows, device):
@@ -227,18 +231,25 @@
     c_copies = [to_row(0, block_n, rows_of(r), 2 * y + 1 - z)]
     col_out[rows_of(r), :] = block_n[...]
 
-    @pl.when(moves)
+    there_sum[...] = total
+
+    @pl.when(elsewhere)
     def _():
         energy = jnp.zeros((1, BLOCK), jnp.float32)
         for k in range(16):
             pltpu.make_async_remote_copy(
                 src_ref=energy_send, dst_ref=there_land.at[k],
                 send_sem=there_send.at[0], recv_sem=there_recv.at[k],
-                device_id=partner, device_id_type=MESH,
+                device_id=target, device_id_type=MESH,
             ).wait_recv()
             energy = energy + there_land[k, 0:1, :]
+        there_sum[...] = energy
+
+    @pl.when(moves)
+    def _():
         t_copy.wait_recv()
-        moved[...] = (decode(t_land) * lax.rsqrt(energy / M + epsilon)).astype(jnp.bfloat16)
+        factor = lax.rsqrt(there_sum[...] / M + epsilon)
+        moved[...] = (decode(t_land) * factor).astype(jnp.bfloat16)
 
     @pl.when(jnp.logical_not(moves))
     def _():
@@ -263,7 +274,7 @@
         c_copies.append(to_row(3 + d, col_out.at[beside, :], beside, 2 * lax.rem(y + d, 4) + z))
     s_copies.append(to_sibling(1, row_out.at[other], other))
     for n, side in enumerate((near, far)):
-        for m, d in enumerate((2, 1, 3)):
+        for m, d in ((1, 1), (2, 3), (0, 2)):
             b_copies[1 + 3 * n + m].wait_recv()
             spot = place(side + lax.rem(x + 4 - d, 4))
             s_copies.append(to_sibling(2 + 3 * n + m, row_out.at[spot], spot))
@@ -303,6 +314,7 @@
             VMEM((8, BLOCK), jnp.float32),
             VMEM((15, 8, BLOCK), jnp.float32),
             VMEM((16, 8, BLOCK), jnp.float32),
+            VMEM((1, BLOCK), jnp.float32),
             VMEM((WIDTH + 16, BLOCK), jnp.int16),
             VMEM((WIDTH + 16, BLOCK), jnp.int16),
             VMEM((BLOCK, WIDTH), jnp.bfloat16),

time: 48 us -> 45.5 us (0.948)
  Pallas kernels: 46.9 us -> 44.6 us
    pallas_call x1, Pallas kernels: 42.7 us -> 40.4 us  [project(): pl.pallas_call(project_kernel, out_shape=(jax.ShapeDtypeStruct((2 * WIDTH...]
where the time goes in v6:
time: 45.5 us; the launch traced here: 45.3 us
  Pallas kernels  44.6 us (98%)
  local copies, waits for them, and re-layouts  0.71 us (2%)
    pallas_call x1, Pallas kernels, project(): pl.pallas_call(project_kernel, out_shape=(jax.ShapeDtypeStruct((2 * WIDTH...  40.4 us
    pallas_call x1, Pallas kernels, correlate(): pl.pallas_call(correlate_kernel, out_shape=jax.ShapeDtypeStruct((LAGS, 2...  4.26 us

profile of v6, /device:TPU:1, one launch (start us, length us, event | category | flops | bytes accessed | tf_op | source)
XLA Modules:
  0.0 45.3 jit_solution(6496342777202725233)
XLA Ops:
  0.0 0.0 copy-start
  0.0 0.7 %copy-done = s32[2560]{0:T(1024)S(1)} copy-done((s32[2560]{0:T(1024)S(1)}, s32[2560]{0:T(1024)}, u32[]{:S(2)}) %copy-start) | copy-done | bytes 10264
  0.7 0.0 copy-start.1
  0.7 40.4 %shard_map.46 = (bf16[512,1024]{1,0:T(8,128)(2,1)S(1)}, bf16[1024,256]{1,0:T(8,128)(2,1)S(1)}) custom-call(s32[2560]{0:T(1024)S(1)} %copy-done, bf16[7680,256]{1,0:T(8,128)(2,1)} %panel_hbm.1, bf16[1024,7680]{1,0:T(8,128)(2,1)} %v_hbm.1), custom_call_target="tpu_custom_call" | custom-call | tf_op jit(solution)/shard_map/pallas_call | solution.py:293
  41.1 0.0 copy-done.1
  41.1 4.3 %shard_map.47 = f32[8,512,256]{2,1,0:T(8,128)} custom-call(s32[8]{0:T(128)S(1)} %copy-done.1, bf16[512,1024]{1,0:T(8,128)(2,1)S(1)} %get-tuple-element.7.rows_ref, bf16[1024,256]{1,0:T(8,128)(2,1)S(1)} %get-tuple-element.8.cols_ref), custom_call_target="tpu_custom_call" | custom-call | tf_op jit(solution)/shard_map/pallas_call | solution.py:361
Async XLA Ops:
  0.0 0.7 %copy-start = (s32[2560]{0:T(1024)S(1)}, s32[2560]{0:T(1024)}, u32[]{:S(2)}) copy-start(s32[2560]{0:T(1024)} %slot_hbm.1) | copy-start | bytes 30724
  0.7 40.4 %copy-start.1 = (s32[8]{0:T(128)S(1)}, s32[8]{0:T(128)}, u32[]{:S(2)}) copy-start(s32[8]{0:T(128)} %lag_ref.1) | copy-start | bytes 100

commit v7 on v6

--- a/solution.py
+++ b/solution.py
@@ -37,10 +37,14 @@
     return ref[:WIDTH, :].astype(jnp.int32).astype(jnp.float32) * (jnp.exp2(power) / FULL)
 
 
+def turn(i):
+    return jnp.where(i == 3, 0, jnp.where(i == 2, 1, i + 2))
+
+
 def project_kernel(
     slot_hbm, panel_hbm, v_hbm, row_out, col_out,
-    slot_ref, panel, wide, ordered, v_buf, part, sent, landed, energy_send, energy_land, there_land, there_sum, t_sent, t_land, block_n, moved,
-    slot_sem, panel_sem, v_sem, rs_send, rs_recv, e_send, e_recv, there_send, there_recv, c_send, c_recv, t_send, t_recv,
+    slot_ref, panel, wide, ordered, v_buf, part, sent, landed, own_send, own_land, energy_send, energy_land, there_land, there_sum, t_sent, t_land, block_n, moved,
+    slot_sem, panel_sem, v_sem, rs_send, rs_recv, pair_send, pair_recv, e_send, e_recv, there_send, there_recv, c_send, c_recv, t_send, t_recv,
     b_send, b_recv, s_send, s_recv,
 ):
     r, c = lax.axis_index("row"), lax.axis_index("col")
@@ -58,7 +62,7 @@
             pltpu.make_async_copy(panel_hbm.at[rows, :], panel.at[rows, :], panel_sem.at[i])
         )
         panel_copies[-1].start()
-    quads = [lax.rem(y + i + 1, 4) for i in range(4)]
+    quads = [lax.rem(y + turn(i), 4) for i in range(4)]
     v_copies = []
     for i, q in enumerate(quads):
         rows = pl.ds(pl.multiple_of(q * 256, 256), 256)
@@ -67,8 +71,11 @@
     barrier = pltpu.get_barrier_semaphore()
     for d in range(1, 8):
         pl.semaphore_signal(barrier, inc=1, device_id=(lax.rem(r + d, 8), c), device_id_type=MESH)
-    for d in range(1, 16):
-        pl.semaphore_signal(barrier, inc=1, device_id=(r, lax.rem(c + d, 16)), device_id_type=MESH)
+    for d in range(1, 8):
+        peer = 2 * lax.rem(chip + d, 8) + core
+        pl.semaphore_signal(barrier, inc=1, device_id=(r, peer), device_id_type=MESH)
+    sibling = (r, 2 * chip + 1 - core)
+    pl.semaphore_signal(barrier, inc=1, device_id=sibling, device_id_type=MESH)
     target = (chip, 2 * lax.rem(r + chip, 8) + core)
     origin = lax.rem(chip + 8 - r, 8)
     moves = (r != 0) | (chip != 0)
@@ -76,8 +83,9 @@
 
     @pl.when(elsewhere)
     def _():
-        for k in range(16):
-            pl.semaphore_signal(barrier, inc=1, device_id=(origin, k), device_id_type=MESH)
+        for k in range(8):
+            peer = 2 * k + core
+            pl.semaphore_signal(barrier, inc=1, device_id=(origin, peer), device_id_type=MESH)
 
     for i in range(CHUNKS):
         panel_copies[i].wait()
@@ -117,7 +125,7 @@
 
     lax.fori_loop(0, ATOMS // UNIT, take, 0)
 
-    pl.semaphore_wait(barrier, 36)
+    pl.semaphore_wait(barrier, 22)
 
     def rs_copy(i, zz):
         to_z = lax.rem(z + 1 + zz, 2)
@@ -125,7 +133,7 @@
         return pltpu.make_async_remote_copy(
             src_ref=sent.at[i, to_z], dst_ref=landed.at[k],
             send_sem=rs_send.at[k], recv_sem=rs_recv.at[k],
-            device_id=(2 * lax.rem(y + i + 1, 4) + to_z, c), device_id_type=MESH,
+            device_id=(2 * lax.rem(y + turn(i), 4) + to_z, c), device_id_type=MESH,
         )
 
     def step(i, _):
@@ -161,31 +169,35 @@
         t_copy.start()
 
     own = jnp.sum(turned * turned, axis=0, keepdims=True)
-    energy_send[...] = jnp.broadcast_to(own, (8, BLOCK))
-    e_copies = []
+    own_send[...] = jnp.broadcast_to(own, (8, BLOCK))
+    pair_copy = pltpu.make_async_remote_copy(
+        src_ref=own_send, dst_ref=own_land, send_sem=pair_send, recv_sem=pair_recv,
+        device_id=sibling, device_id_type=MESH,
+    )
+    pair_copy.start()
+    pair_copy.wait_recv()
+    total = own + own_land[0:1, :]
+    energy_send[...] = jnp.broadcast_to(total, (8, BLOCK))
+    e_copies = [pair_copy]
+    own_copies = []
     for d in range(1, 8):
-        to_row_of = lax.rem(r + d, 8)
-        for k in range(2):
-            n = 2 * (d - 1) + k
-            copy = pltpu.make_async_remote_copy(
-                src_ref=energy_send, dst_ref=there_land.at[c],
-                send_sem=there_send.at[n], recv_sem=there_recv.at[c],
-                device_id=(to_row_of, 2 * lax.rem(to_row_of + r, 8) + k), device_id_type=MESH,
-            )
-            copy.start()
-            e_copies.append(copy)
-    own_copies = []
-    for d in range(1, 16):
         copy = pltpu.make_async_remote_copy(
             src_ref=energy_send, dst_ref=energy_land.at[d - 1],
             send_sem=e_send.at[d - 1], recv_sem=e_recv.at[d - 1],
-            device_id=(r, lax.rem(c + d, 16)), device_id_type=MESH,
+            device_id=(r, 2 * lax.rem(chip + d, 8) + core), device_id_type=MESH,
         )
         copy.start()
         own_copies.append(copy)
+        to_row_of = lax.rem(r + d, 8)
+        copy = pltpu.make_async_remote_copy(
+            src_ref=energy_send, dst_ref=there_land.at[chip],
+            send_sem=there_send.at[d - 1], recv_sem=there_recv.at[chip],
+            device_id=(to_row_of, 2 * lax.rem(to_row_of + r, 8) + core), device_id_type=MESH,
+        )
+        copy.start()
+        e_copies.append(copy)
     e_copies += own_copies
-    total = own
-    for d in range(15):
+    for d in range(7):
         own_copies[d].wait_recv()
         total = total + energy_land[d, 0:1, :]
     scaled = turned * lax.rsqrt(total / M + epsilon)
@@ -223,7 +235,7 @@
         copy = pltpu.make_async_remote_copy(
             src_ref=src, dst_ref=row_out.at[spot],
             send_sem=s_send.at[k], recv_sem=s_recv.at[k],
-            device_id=(r, 2 * chip + 1 - core), device_id_type=MESH,
+            device_id=sibling, device_id_type=MESH,
         )
         copy.start()
         return copy
@@ -236,7 +248,7 @@
     @pl.when(elsewhere)
     def _():
         energy = jnp.zeros((1, BLOCK), jnp.float32)
-        for k in range(16):
+        for k in range(8):
             pltpu.make_async_remote_copy(
                 src_ref=energy_send, dst_ref=there_land.at[k],
                 send_sem=there_send.at[0], recv_sem=there_recv.at[k],
@@ -312,8 +324,10 @@
             VMEM((4, 2, WIDTH + 16, BLOCK), jnp.int16),
             VMEM((7, WIDTH + 16, BLOCK), jnp.int16),
             VMEM((8, BLOCK), jnp.float32),
-            VMEM((15, 8, BLOCK), jnp.float32),
-            VMEM((16, 8, BLOCK), jnp.float32),
+            VMEM((8, BLOCK), jnp.float32),
+            VMEM((8, BLOCK), jnp.float32),
+            VMEM((7, 8, BLOCK), jnp.float32),
+            VMEM((8, 8, BLOCK), jnp.float32),
             VMEM((1, BLOCK), jnp.float32),
             VMEM((WIDTH + 16, BLOCK), jnp.int16),
             VMEM((WIDTH + 16, BLOCK), jnp.int16),
@@ -321,8 +335,9 @@
             VMEM((WIDTH, BLOCK), jnp.bfloat16),
             DMA, DMA((CHUNKS,)), DMA((4,)),
             DMA((7,)), DMA((7,)),
-            DMA((15,)), DMA((15,)),
-            DMA((14,)), DMA((16,)),
+            DMA, DMA,
+            DMA((7,)), DMA((7,)),
+            DMA((7,)), DMA((8,)),
             DMA((7,)), DMA((7,)),
             DMA, DMA,
             DMA((7,)), DMA((7,)),

time: 45.5 us -> 44.2 us (0.971)
  Pallas kernels: 44.6 us -> 43.3 us
    pallas_call x1, Pallas kernels: 40.4 us -> 39 us  [project(): pl.pallas_call(project_kernel, out_shape=(jax.ShapeDtypeStruct((2 * WIDTH...]
where the time goes in v7:
time: 44.2 us; the launch traced here: 44 us
  Pallas kernels  43.3 us (98%)
  local copies, waits for them, and re-layouts  0.71 us (2%)
    pallas_call x1, Pallas kernels, project(): pl.pallas_call(project_kernel, out_shape=(jax.ShapeDtypeStruct((2 * WIDTH...  39 us
    pallas_call x1, Pallas kernels, correlate(): pl.pallas_call(correlate_kernel, out_shape=jax.ShapeDtypeStruct((LAGS, 2...  4.24 us

profile of v7, /device:TPU:1, one launch (start us, length us, event | category | flops | bytes accessed | tf_op | source)
XLA Modules:
  0.0 44.0 jit_solution(9178496416797268714)
XLA Ops:
  0.0 0.0 copy-start
  0.0 0.7 %copy-done = s32[2560]{0:T(1024)S(1)} copy-done((s32[2560]{0:T(1024)S(1)}, s32[2560]{0:T(1024)}, u32[]{:S(2)}) %copy-start) | copy-done | bytes 10264
  0.7 0.0 copy-start.1
  0.7 39.0 %shard_map.46 = (bf16[512,1024]{1,0:T(8,128)(2,1)S(1)}, bf16[1024,256]{1,0:T(8,128)(2,1)S(1)}) custom-call(s32[2560]{0:T(1024)S(1)} %copy-done, bf16[7680,256]{1,0:T(8,128)(2,1)} %panel_hbm.1, bf16[1024,7680]{1,0:T(8,128)(2,1)} %v_hbm.1), custom_call_target="tpu_custom_call" | custom-call | tf_op jit(solution)/shard_map/pallas_call | solution.py:305
  39.8 0.0 copy-done.1
  39.8 4.2 %shard_map.47 = f32[8,512,256]{2,1,0:T(8,128)} custom-call(s32[8]{0:T(128)S(1)} %copy-done.1, bf16[512,1024]{1,0:T(8,128)(2,1)S(1)} %get-tuple-element.7.rows_ref, bf16[1024,256]{1,0:T(8,128)(2,1)S(1)} %get-tuple-element.8.cols_ref), custom_call_target="tpu_custom_call" | custom-call | tf_op jit(solution)/shard_map/pallas_call | solution.py:376
Async XLA Ops:
  0.0 0.7 %copy-start = (s32[2560]{0:T(1024)S(1)}, s32[2560]{0:T(1024)}, u32[]{:S(2)}) copy-start(s32[2560]{0:T(1024)} %slot_hbm.1) | copy-start | bytes 30724
  0.7 39.0 %copy-start.1 = (s32[8]{0:T(128)S(1)}, s32[8]{0:T(128)}, u32[]{:S(2)}) copy-start(s32[8]{0:T(128)} %lag_ref.1) | copy-start | bytes 100

commit v8 on v7

--- a/solution.py
+++ b/solution.py
@@ -13,7 +13,7 @@
 ROWS = 3 * ATOMS
 WIDTH = 256
 BLOCK = 128
-CHUNKS = 4
+CHUNKS = 8
 UNIT = 16
 TINY = 1e-30
 FULL = 32760.0
@@ -127,46 +127,44 @@
 
     pl.semaphore_wait(barrier, 22)
 
-    def rs_copy(i, zz):
+    def rs_copy(k):
+        to_z = lax.rem(z + 1 + lax.rem(k, 2), 2)
+        return pltpu.make_async_remote_copy(
+            src_ref=sent.at[k], dst_ref=landed.at[k],
+            send_sem=rs_send.at[k], recv_sem=rs_recv.at[k],
+            device_id=(2 * lax.rem(y + turn(k // 2), 4) + to_z, c), device_id_type=MESH,
+        )
+
+    def step(i, _):
+        quad, zz = i // 2, lax.rem(i, 2)
         to_z = lax.rem(z + 1 + zz, 2)
-        k = 2 * i + zz
-        return pltpu.make_async_remote_copy(
-            src_ref=sent.at[i, to_z], dst_ref=landed.at[k],
-            send_sem=rs_send.at[k], recv_sem=rs_recv.at[k],
-            device_id=(2 * lax.rem(y + turn(i), 4) + to_z, c), device_id_type=MESH,
-        )
-
-    def step(i, _):
-        pltpu.make_async_copy(v_hbm.at[pl.ds(0, 256), :], v_buf.at[i], v_sem.at[i]).wait()
-        part[i] = jnp.dot(v_buf[i], ordered[...], preferred_element_type=jnp.float32)
-        for zz in range(2):
-            coded, powers = code(part[i, zz * BLOCK : (zz + 1) * BLOCK, :].T)
-            sent[i, zz, :WIDTH, :] = coded
-            sent[i, zz, WIDTH:, :] = powers
-        rs_copy(i, 0).start()
-
-        @pl.when(i < 3)
+
+        @pl.when(zz == 0)
         def _():
-            rs_copy(i, 1).start()
+            pltpu.make_async_copy(
+                v_hbm.at[pl.ds(0, 256), :], v_buf.at[quad], v_sem.at[quad]
+            ).wait()
+
+        rows = pl.ds(pl.multiple_of(to_z * BLOCK, BLOCK), BLOCK)
+        part[...] = jnp.dot(
+            v_buf[quad, rows, :], ordered[...], preferred_element_type=jnp.float32
+        )
+        coded, powers = code(part[...].T)
+        sent[i, :WIDTH, :] = coded
+        sent[i, WIDTH:, :] = powers
+
+        @pl.when(i < 7)
+        def _():
+            rs_copy(i).start()
 
         return 0
 
-    lax.fori_loop(0, 4, step, 0)
-    rs_copies = [rs_copy(k // 2, k % 2) for k in range(7)]
-    turned = part[3, pl.ds(pl.multiple_of(z * BLOCK, BLOCK), BLOCK), :].T
+    lax.fori_loop(0, 8, step, 0)
+    rs_copies = [rs_copy(k) for k in range(7)]
+    turned = part[...].T
     for k in range(7):
         rs_copies[k].wait_recv()
         turned = turned + decode(landed.at[k])
-
-    t_sent[:WIDTH, :], t_sent[WIDTH:, :] = code(turned)
-    t_copy = pltpu.make_async_remote_copy(
-        src_ref=t_sent, dst_ref=t_land, send_sem=t_send, recv_sem=t_recv,
-        device_id=target, device_id_type=MESH,
-    )
-
-    @pl.when(moves)
-    def _():
-        t_copy.start()
 
     own = jnp.sum(turned * turned, axis=0, keepdims=True)
     own_send[...] = jnp.broadcast_to(own, (8, BLOCK))
@@ -175,6 +173,17 @@
         device_id=sibling, device_id_type=MESH,
     )
     pair_copy.start()
+
+    t_sent[:WIDTH, :], t_sent[WIDTH:, :] = code(turned)
+    t_copy = pltpu.make_async_remote_copy(
+        src_ref=t_sent, dst_ref=t_land, send_sem=t_send, recv_sem=t_recv,
+        device_id=target, device_id_type=MESH,
+    )
+
+    @pl.when(moves)
+    def _():
+        t_copy.start()
+
     pair_copy.wait_recv()
     total = own + own_land[0:1, :]
     energy_send[...] = jnp.broadcast_to(total, (8, BLOCK))
@@ -269,12 +278,12 @@
 
     far = 4 * (1 - zh)
     near = 4 * zh
+    s_copies = [to_sibling(0, moved, place(chip))]
     b_copies = [to_col(0, moved, place(chip), far + x)]
     for d in (2, 1, 3):
         b_copies.append(to_col(d, moved, place(chip), near + lax.rem(x + d, 4)))
     for d in (2, 1, 3):
         c_copies.append(to_row(d, block_n, rows_of(r), 2 * lax.rem(y + d, 4) + z))
-    s_copies = [to_sibling(0, moved, place(chip))]
     row_out[place(chip)] = moved[...]
     b_copies[0].wait_recv()
     other = place(far + x)
@@ -320,8 +329,8 @@
             VMEM((2, ROWS + 16, 128), jnp.float32),
             VMEM((ROWS, WIDTH), jnp.bfloat16),
             VMEM((4, 256, ROWS), jnp.bfloat16),
-            VMEM((4, 2 * BLOCK, WIDTH), jnp.float32),
-            VMEM((4, 2, WIDTH + 16, BLOCK), jnp.int16),
+            VMEM((BLOCK, WIDTH), jnp.float32),
+            VMEM((8, WIDTH + 16, BLOCK), jnp.int16),
             VMEM((7, WIDTH + 16, BLOCK), jnp.int16),
             VMEM((8, BLOCK), jnp.float32),
             VMEM((8, BLOCK), jnp.float32),

time: 44.2 us -> 43.9 us (level)
  no operation moved by 1% of the time
where the time goes in v8:
time: 43.9 us; the launch traced here: 43.8 us
  Pallas kernels  43 us (98%)
  local copies, waits for them, and re-layouts  0.71 us (2%)
    pallas_call x1, Pallas kernels, project(): pl.pallas_call(project_kernel, out_shape=(jax.ShapeDtypeStruct((2 * WIDTH...  38.8 us
    pallas_call x1, Pallas kernels, correlate(): pl.pallas_call(correlate_kernel, out_shape=jax.ShapeDtypeStruct((LAGS, 2...  4.26 us

profile of v8, /device:TPU:1, one launch (start us, length us, event | category | flops | bytes accessed | tf_op | source)
XLA Modules:
  0.0 43.8 jit_solution(14103670741201875074)
XLA Ops:
  0.0 0.0 copy-start
  0.0 0.7 %copy-done = s32[2560]{0:T(1024)S(1)} copy-done((s32[2560]{0:T(1024)S(1)}, s32[2560]{0:T(1024)}, u32[]{:S(2)}) %copy-start) | copy-done | bytes 10264
  0.7 0.0 copy-start.1
  0.7 38.8 %shard_map.46 = (bf16[512,1024]{1,0:T(8,128)(2,1)S(1)}, bf16[1024,256]{1,0:T(8,128)(2,1)S(1)}) custom-call(s32[2560]{0:T(1024)S(1)} %copy-done, bf16[7680,256]{1,0:T(8,128)(2,1)} %panel_hbm.1, bf16[1024,7680]{1,0:T(8,128)(2,1)} %v_hbm.1), custom_call_target="tpu_custom_call" | custom-call | tf_op jit(solution)/shard_map/pallas_call | solution.py:314
  39.5 0.0 copy-done.1
  39.5 4.3 %shard_map.47 = f32[8,512,256]{2,1,0:T(8,128)} custom-call(s32[8]{0:T(128)S(1)} %copy-done.1, bf16[512,1024]{1,0:T(8,128)(2,1)S(1)} %get-tuple-element.7.rows_ref, bf16[1024,256]{1,0:T(8,128)(2,1)S(1)} %get-tuple-element.8.cols_ref), custom_call_target="tpu_custom_call" | custom-call | tf_op jit(solution)/shard_map/pallas_call | solution.py:385
Async XLA Ops:
  0.0 0.7 %copy-start = (s32[2560]{0:T(1024)S(1)}, s32[2560]{0:T(1024)}, u32[]{:S(2)}) copy-start(s32[2560]{0:T(1024)} %slot_hbm.1) | copy-start | bytes 30724
  0.7 38.8 %copy-start.1 = (s32[8]{0:T(128)S(1)}, s32[8]{0:T(128)}, u32[]{:S(2)}) copy-start(s32[8]{0:T(128)} %lag_ref.1) | copy-start | bytes 100

commit v9 on v8

--- a/solution.py
+++ b/solution.py
@@ -375,8 +375,11 @@
                 rows_ref[rows, :], shifted[i % 2], preferred_element_type=jnp.float32
             )
             held[i, rows, :] = product * factor
-        copies.append(pltpu.make_async_copy(held.at[i], out_hbm.at[i], out_sem.at[i]))
-        copies[-1].start()
+            copy = pltpu.make_async_copy(
+                held.at[i, rows, :], out_hbm.at[i, rows, :], out_sem.at[2 * i + p]
+            )
+            copy.start()
+            copies.append(copy)
     for copy in copies:
         copy.wait()
 
@@ -395,7 +398,7 @@
             VMEM((2, S + MAXLAG, 128), jnp.float32),
             VMEM((2, S, WIDTH), jnp.bfloat16),
             VMEM((LAGS, 2 * WIDTH, WIDTH), jnp.float32),
-            DMA((LAGS,)),
+            DMA((2 * LAGS,)),
         ],
         compiler_params=pltpu.CompilerParams(vmem_limit_bytes=24 * 2**20),
     )(lag_offsets, row_modes, column_modes)

time: 43.9 us -> 44 us (level)
  no operation moved by 1% of the time
where the time goes in v9:
time: 44 us; the launch traced here: 43.8 us
  Pallas kernels  43.1 us (98%)
  local copies, waits for them, and re-layouts  0.71 us (2%)
    pallas_call x1, Pallas kernels, project(): pl.pallas_call(project_kernel, out_shape=(jax.ShapeDtypeStruct((2 * WIDTH...  38.8 us
    pallas_call x1, Pallas kernels, correlate(): pl.pallas_call(correlate_kernel, out_shape=jax.ShapeDtypeStruct((LAGS, 2...  4.35 us

profile of v9, /device:TPU:1, one launch (start us, length us, event | category | flops | bytes accessed | tf_op | source)
XLA Modules:
  0.0 43.8 jit_solution(351052181089762140)
XLA Ops:
  0.0 0.0 copy-start
  0.0 0.7 %copy-done = s32[2560]{0:T(1024)S(1)} copy-done((s32[2560]{0:T(1024)S(1)}, s32[2560]{0:T(1024)}, u32[]{:S(2)}) %copy-start) | copy-done | bytes 10264
  0.7 0.0 copy-start.1
  0.7 38.8 %shard_map.46 = (bf16[512,1024]{1,0:T(8,128)(2,1)S(1)}, bf16[1024,256]{1,0:T(8,128)(2,1)S(1)}) custom-call(s32[2560]{0:T(1024)S(1)} %copy-done, bf16[7680,256]{1,0:T(8,128)(2,1)} %panel_hbm.1, bf16[1024,7680]{1,0:T(8,128)(2,1)} %v_hbm.1), custom_call_target="tpu_custom_call" | custom-call | tf_op jit(solution)/shard_map/pallas_call | solution.py:314
  39.5 0.0 copy-done.1
  39.5 4.4 %shard_map.47 = f32[8,512,256]{2,1,0:T(8,128)} custom-call(s32[8]{0:T(128)S(1)} %copy-done.1, bf16[512,1024]{1,0:T(8,128)(2,1)S(1)} %get-tuple-element.7.rows_ref, bf16[1024,256]{1,0:T(8,128)(2,1)S(1)} %get-tuple-element.8.cols_ref), custom_call_target="tpu_custom_call" | custom-call | tf_op jit(solution)/shard_map/pallas_call | solution.py:388
Async XLA Ops:
  0.0 0.7 %copy-start = (s32[2560]{0:T(1024)S(1)}, s32[2560]{0:T(1024)}, u32[]{:S(2)}) copy-start(s32[2560]{0:T(1024)} %slot_hbm.1) | copy-start | bytes 30724
  0.7 38.8 %copy-start.1 = (s32[8]{0:T(128)S(1)}, s32[8]{0:T(128)}, u32[]{:S(2)}) copy-start(s32[8]{0:T(128)} %lag_ref.1) | copy-start | bytes 100
